TPU v7x, 256 devices: a whole 4x4x8 slice. The times are simulated.
256 devices in a mesh: depth: 16 (over z, core), lat: 16 (over x, y).
Axes of the slice: x: 4, y: 4, z: 8, core: 2. Of those that a mesh axis runs over, the one named last changes fastest.
Arguments:
- volume: bfloat16 [256, 512, 2048], P('depth', 'lat'), may hold values from -6 to 6
- labels: int32 [256, 512, 2048], P('depth', 'lat'), may hold values from 0 to 7
- active_slices: int32 [16, 16], P('depth', 'lat'), may hold values from 0 to 16, as said below
- view_order: int32 [16], replicated, may hold values from 0 to 15, each once
- density_gain: float32 [8], replicated, may hold values from 0.5 to 3
- density_bias: float32 [8], replicated, may hold values from -2 to 1
- albedo_table: float32 [3, 8], replicated, may hold values from 0.1 to 1
- motion_table: float32 [2, 8], replicated, may hold values from -4 to 4
- conv_first: bfloat16 [3, 3, 32, 20], replicated, may hold values from -0.4375 to 0.4375
- bias_first: float32 [32], replicated, may hold values from -3 to 3
- conv_second: bfloat16 [3, 3, 3, 32], replicated, may hold values from -0.375 to 0.375
- bias_second: float32 [3], replicated, may hold values from -3 to 3
Outputs:
- aovs: float32 [20, 512, 2048], P(None, 'lat', 'depth')
- denoised: float32 [3, 512, 2048], P(None, 'lat', 'depth')
Inputs may be any that keep to these rules, and one draw needn't show every extreme that they name: A brick has data only in its first active_slices[slab, band] slices; 0 marks an empty brick, and some brick is full. `view_order`: each slab appears once.
All inputs are finite; a program needn't handle non-finite values.
Results may differ from a plain program's by a relative error of at most 0.0031.
Values may be sent and summed in bfloat16 or wider, within the bound.
A program may use at most 128 MiB of HBM per device.

v0:
```python
import jax
import jax.numpy as jnp
from jax import lax
from jax.sharding import PartitionSpec as P


def padded_2(shard, sides, width):
    for axis, dim in sides:
        count, length = (lax.axis_size(axis), shard.shape[dim])
        up = [(i, (i + 1) % count) for i in range(count - 1)]
        down = [(j, i) for i, j in up]
        last = lax.slice_in_dim(shard, length - width, length, axis=dim)
        first = lax.slice_in_dim(shard, 0, width, axis=dim)
        before = lax.ppermute(last, axis, up)
        after = lax.ppermute(first, axis, down)
        shard = jnp.concatenate([before, shard, after], axis=dim)
    return shard


def render_plane(
    lower_plane,
    middle_plane,
    upper_plane,
    classes,
    active,
    offset,
    density_gain,
    density_bias,
    albedo_table,
    motion_table,
    optical,
):
    center = middle_plane[1:-1, 1:-1].astype(jnp.float32)
    below = lower_plane[1:-1, 1:-1].astype(jnp.float32)
    above = upper_plane[1:-1, 1:-1].astype(jnp.float32)
    grad_x = (
        middle_plane[1:-1, 2:].astype(jnp.float32) - middle_plane[1:-1, :-2].astype(jnp.float32)
    ) * 0.5
    grad_y = (
        middle_plane[2:, 1:-1].astype(jnp.float32) - middle_plane[:-2, 1:-1].astype(jnp.float32)
    ) * 0.5
    grad_z = (above - below) * 0.5
    inverse_norm = lax.rsqrt(grad_x * grad_x + grad_y * grad_y + grad_z * grad_z + 1.0)
    normal = jnp.stack([grad_x * inverse_norm, grad_y * inverse_norm, grad_z * inverse_norm], 0)
    class_count = density_gain.shape[0]
    onehot = (classes[None] == jnp.arange(class_count, dtype=jnp.int32)[:, None, None]).astype(
        jnp.float32
    )
    gain_map = jnp.sum(density_gain[:, None, None] * onehot, 0)
    bias_map = jnp.sum(density_bias[:, None, None] * onehot, 0)
    density = jax.nn.softplus(gain_map * center + bias_map)
    opacity = (1.0 - jnp.exp(-optical * density)) * active
    shading = 0.4 + 0.6 * jnp.maximum(0.48 * normal[0] + 0.6 * normal[1] + 0.64 * normal[2], 0.0)
    texture = 0.55 + 0.45 * jnp.tanh(below + above)
    albedo = jnp.sum(albedo_table[:, :, None, None] * onehot[None], 1) * texture[None]
    motion = (
        jnp.sum(motion_table[:, :, None, None] * onehot[None], 1)
        * (1.0 + 0.5 * jnp.tanh(center))[None]
    )
    feature = jnp.concatenate(
        [albedo * shading[None], jnp.ones_like(center)[None], normal, albedo, onehot, motion], 0
    )
    contrib = opacity[None] * feature
    columns = contrib.shape[2]
    widened = jnp.pad(contrib, ((0, 0), (0, 0), (columns, 0)))
    return lax.dynamic_slice_in_dim(widened, columns - offset, columns, 2)


def convolve(padded, weight, row_count, col_count):
    result = jnp.zeros((weight.shape[2], row_count, col_count), jnp.float32)
    for row_tap in range(3):
        for col_tap in range(3):
            window = padded[:, row_tap : row_tap + row_count, col_tap : col_tap + col_count]
            result = result + jnp.einsum(
                "oc,crq->orq", weight[row_tap, col_tap], window, preferred_element_type=jnp.float32
            )
    return result


def front_products(ordered):
    remaining = 1.0 - ordered.astype(jnp.float32)
    through = jnp.cumprod(remaining, 0)
    return jnp.concatenate([jnp.ones_like(through[:1]), through[:-1]], 0)


def per_device(
    volume,
    labels,
    active_slices,
    view_order,
    density_gain,
    density_bias,
    albedo_table,
    motion_table,
    conv_first,
    bias_first,
    conv_second,
    bias_second,
):
    slices, row_count, columns = volume.shape
    depth_count = lax.axis_size("depth")
    optical = 2.0 / (depth_count * slices)
    channels = 12 + density_gain.shape[0]
    padded = padded_2(volume, (("depth", 0), ("lat", 1)), 1)
    padded = jnp.pad(padded, ((0, 0), (0, 0), (1, 1)))
    first_slice = lax.axis_index("depth") * slices

    def advance(slice_index, accum_state):
        lower_plane = lax.dynamic_index_in_dim(padded, slice_index, 0, keepdims=False)
        middle_plane = lax.dynamic_index_in_dim(padded, slice_index + 1, 0, keepdims=False)
        upper_plane = lax.dynamic_index_in_dim(padded, slice_index + 2, 0, keepdims=False)
        classes = lax.dynamic_index_in_dim(labels, slice_index, 0, keepdims=False)
        offset = (first_slice + slice_index) // 4
        contrib = render_plane(
            lower_plane,
            middle_plane,
            upper_plane,
            classes,
            1.0,
            offset,
            density_gain,
            density_bias,
            albedo_table,
            motion_table,
            optical,
        )
        return accum_state + (1.0 - accum_state[3])[None] * contrib

    final = lax.fori_loop(
        0, active_slices[0, 0], advance, jnp.zeros((channels, row_count, columns), jnp.float32)
    )
    partial_value = final.astype(jnp.bfloat16)
    ordered = jnp.take(
        lax.all_to_all(partial_value[None], "depth", split_axis=3, concat_axis=0, tiled=True),
        view_order,
        axis=0,
    )
    before = front_products(ordered[:, 3])
    aovs = jnp.sum(ordered.astype(jnp.float32) * before[:, None], 0)
    tile_cols = aovs.shape[2]
    features = aovs.astype(jnp.bfloat16)
    feature_pad = padded_2(features, (("depth", 2), ("lat", 1)), 1)
    hidden = jnp.maximum(
        convolve(feature_pad, conv_first, row_count, tile_cols) + bias_first[:, None, None], 0.0
    ).astype(jnp.bfloat16)
    hidden_pad = padded_2(hidden, (("depth", 2), ("lat", 1)), 1)
    denoised = (
        aovs[0:3]
        + convolve(hidden_pad, conv_second, row_count, tile_cols)
        + bias_second[:, None, None]
    )
    return (aovs, denoised)


def solution(mesh):
    placed = (
        P("depth", "lat", None),
        P("depth", "lat", None),
        P("depth", "lat"),
        P(),
        P(),
        P(),
        P(),
        P(),
        P(),
        P(),
        P(),
        P(),
    )
    return jax.shard_map(
        per_device,
        mesh=mesh,
        in_specs=placed,
        out_specs=(P(None, "lat", "depth"), P(None, "lat", "depth")),
        check_vma=False,
    )
```

profile of v0, /device:TPU:1, one launch (start us, length us, event | category | flops | bytes accessed | tf_op | source)
XLA Modules:
  0.0 416.8 jit_solution(9641366701396351434)
XLA Ops:
  0.6 1.0 fusion.120
  1.6 4.9 %collective-permute-start = (bf16[1,32,2048]{2,1,0:T(8,128)(2,1)S(1)}, bf16[1,32,2048]{2,1,0:T(8,128)(2,1)S(1)}, u32[]{:S(2)}, u32[]{:S(2)}) collective-permute-start(bf16[1,32,2048]{2,1,0:T(8,128)(2,1)S(1)} %get-tuple-element.179), channel_id=1, source_target_pairs={{0,16},{16,32},{32,48},{48,64},{64,80},{80,96},{96,112},{112,128},... | collective-permute-start | bytes 393224 | tf_op jit(solution)/shard_map/ppermute | solution.py:14
  6.6 1.9 collective-permute-start.1
  8.5 1.7 constant_dynamic-update-slice_fusion.1
  10.3 2.6 collective-permute-done.1
  12.9 1.4 copy-done.1
  14.5 3.2 collective-permute-start.2
  17.8 1.3 collective-permute-start.3
  19.1 0.8 collective-permute-done.2
  19.8 3.8 collective-permute-done.3
  23.6 4.6 %fusion.22 = bf16[18,34,2050]{2,1,0:T(8,128)(2,1)S(1)} fusion(bf16[18,1,2048]{2,1,0:T(2,128)(2,1)S(1)} %collective-permute-done.3, bf16[18,32,2048]{2,1,0:T(8,128)(2,1)} %copy-done.1, bf16[18,1,2048]{2,1,0:T(2,128)(2,1)S(1)} %collective-permute-done.2), kind=kLoop, calls=%fused_computation.55 | loop fusion | flops 15055200 | bytes 5015952 | tf_op jit(solution)/shard_map/concatenate | solution.py:16
  28.3 2.9 broadcast_in_dim.14
  31.3 0.7 while.12
  31.9 13.9 %copy.27 = bf16[20,32,2048]{1,0,2:T(8,128)(2,1)} copy(f32[20,32,2048]{2,1,0:T(8,128)} %get-tuple-element.135) | data formatting | bytes 7864320 | tf_op jit(solution)/shard_map/while | solution.py:129
  45.8 10.5 %bitcast_bitcast_fusion = bf16[2048,1,20,32]{3,2,1,0:T(8,128)(2,1)} fusion(bf16[20,32,2048]{1,0,2:T(8,128)(2,1)} %copy.27), kind=kLoop, calls=%fused_computation.182 | loop fusion | bytes 5242880
  56.3 16.2 %reshape.54 = bf16[16,2,40960]{2,1,0:T(2,128)(2,1)} reshape(bf16[2048,1,20,32]{3,2,1,0:T(8,128)(2,1)} %bitcast_bitcast_fusion) | data formatting | bytes 5242880
  72.5 192.0 %all-to-all-start = ((bf16[16,2,40960]{2,1,0:T(2,128)(2,1)}), bf16[16,2,40960]{2,1,0:T(2,128)(2,1)S(1)}, u32[]{:S(2)}, u32[]{:S(2)}) async-start(bf16[16,2,40960]{2,1,0:T(2,128)(2,1)} %reshape.54), calls=%async_computation | async-start | bytes 5242880 | tf_op jit(solution)/shard_map/all_to_all | solution.py:134
  264.5 59.8 %all-to-all-done = bf16[16,2,40960]{2,1,0:T(2,128)(2,1)S(1)} async-done(((bf16[16,2,40960]{2,1,0:T(2,128)(2,1)}), bf16[16,2,40960]{2,1,0:T(2,128)(2,1)S(1)}, u32[]{:S(2)}, u32[]{:S(2)}) %all-to-all-start) | async-done | bytes 2621472 | tf_op jit(solution)/shard_map/all_to_all | solution.py:134
  324.3 13.1 %reshape.55 = bf16[2048,1,20,32]{3,2,1,0:T(8,128)(2,1)} reshape(bf16[16,2,40960]{2,1,0:T(2,128)(2,1)S(1)} %all-to-all-done) | data formatting | bytes 5242880
  337.4 12.3 %copy.29 = bf16[1,20,32,16,128]{4,2,1,3,0:T(8,128)(2,1)} copy(bf16[1,20,32,16,128]{2,1,4,3,0:T(8,128)(2,1)} %bitcast.145) | data formatting | bytes 5242880 | tf_op jit(solution)/shard_map/all_to_all | solution.py:134
  349.7 2.8 gather_fusion
  352.5 0.3 broadcast_select_fusion
  352.9 0.8 multiply_reduce_fusion.2
  354.0 2.4 collective-permute-start.4
  356.4 2.0 collective-permute-start.5
  359.0 4.4 %collective-permute-done.5 = bf16[20,32,1]{2,0,1:T(8,128)(2,1)S(1)} collective-permute-done((bf16[20,32,1]{2,0,1:T(8,128)(2,1)S(1)}, bf16[20,32,1]{2,0,1:T(8,128)(2,1)S(1)}, u32[]{:S(2)}, u32[]{:S(2)}) %collective-permute-start.5) | collective-permute-done | bytes 1312 | tf_op jit(solution)/shard_map/ppermute | solution.py:15
  363.5 22.9 %collective-permute-start.6 = (bf16[20,1,130]{2,0,1:T(8,128)(2,1)S(1)}, bf16[20,1,130]{2,0,1:T(8,128)(2,1)S(1)}, u32[]{:S(2)}, u32[]{:S(2)}) collective-permute-start(bf16[20,1,130]{2,0,1:T(8,128)(2,1)S(1)} %get-tuple-element.186), channel_id=1, source_target_pairs={{0,1},{1,2},{2,3},{3,4},{4,5},{5,6},{6,7},{7,8},{8,9},{9,10},{10,1... | collective-permute-start | bytes 15608 | tf_op jit(solution)/shard_map/ppermute | solution.py:14
  386.3 1.3 collective-permute-start.7
  387.6 0.3 fusion.67
  387.9 2.8 collective-permute-done.7
  390.8 0.4 maximum_maximum_fusion.1
  391.2 0.3 fusion.69
  391.5 0.3 fusion.71
  391.8 0.3 fusion.60
  392.1 0.3 fusion.62
  392.4 0.3 fusion.64
  392.7 0.4 fusion.30
  393.1 0.4 fusion.32
  393.6 3.2 collective-permute-start.8
  396.8 1.9 collective-permute-start.9
  398.9 1.2 collective-permute-done.8
  400.1 4.4 %collective-permute-done.9 = bf16[32,32,1]{2,0,1:T(8,128)(2,1)S(1)} collective-permute-done((bf16[32,32,1]{2,0,1:T(8,128)(2,1)S(1)}, bf16[32,32,1]{2,0,1:T(8,128)(2,1)S(1)}, u32[]{:S(2)}, u32[]{:S(2)}) %collective-permute-start.9) | collective-permute-done | bytes 2080 | tf_op jit(solution)/shard_map/ppermute | solution.py:15
  404.6 4.6 %collective-permute-start.10 = (bf16[32,1,130]{2,0,1:T(8,128)(2,1)S(1)}, bf16[32,1,130]{2,0,1:T(8,128)(2,1)S(1)}, u32[]{:S(2)}, u32[]{:S(2)}) collective-permute-start(bf16[32,1,130]{2,0,1:T(8,128)(2,1)S(1)} %get-tuple-element.182), channel_id=1, source_target_pairs={{0,1},{1,2},{2,3},{3,4},{4,5},{5,6},{6,7},{7,8},{8,9},{9,10},{10,1... | collective-permute-start | bytes 24968 | tf_op jit(solution)/shard_map/ppermute | solution.py:14
  409.2 1.3 collective-permute-start.11
  410.8 3.2 collective-permute-done.11
  414.0 0.5 maximum_maximum_fusion
  415.8 0.3 fusion.38
  416.2 0.6 copy.32
  (49 shorter events, 3.4 us)
Async XLA Ops:
  1.6 6.9 %collective-permute-start = (bf16[1,32,2048]{2,1,0:T(8,128)(2,1)S(1)}, bf16[1,32,2048]{2,1,0:T(8,128)(2,1)S(1)}, u32[]{:S(2)}, u32[]{:S(2)}) collective-permute-start(bf16[1,32,2048]{2,1,0:T(8,128)(2,1)S(1)} %get-tuple-element.179), channel_id=1, source_target_pairs={{0,16},{16,32},{32,48},{48,64},{64,80},{80,96},{96,112},{112,128},... | collective-permute-start | bytes 393224 | tf_op jit(solution)/shard_map/ppermute | solution.py:14
  6.6 6.3 %collective-permute-start.1 = (bf16[1,32,2048]{2,1,0:T(8,128)(2,1)S(1)}, bf16[1,32,2048]{2,1,0:T(8,128)(2,1)S(1)}, u32[]{:S(2)}, u32[]{:S(2)}) collective-permute-start(bf16[1,32,2048]{2,1,0:T(8,128)(2,1)S(1)} %get-tuple-element.178), channel_id=1, source_target_pairs={{16,0},{32,16},{48,32},{64,48},{80,64},{96,80},{112,96},{128,112},... | collective-permute-start | bytes 393224 | tf_op jit(solution)/shard_map/ppermute | solution.py:15
  12.9 1.4 copy-start.1
  14.5 5.3 %collective-permute-start.2 = (bf16[18,1,2048]{2,1,0:T(2,128)(2,1)S(1)}, bf16[18,1,2048]{2,1,0:T(2,128)(2,1)S(1)}, u32[]{:S(2)}, u32[]{:S(2)}) collective-permute-start(bf16[18,1,2048]{2,1,0:T(2,128)(2,1)S(1)} %get-tuple-element.176), channel_id=1, source_target_pairs={{0,1},{1,2},{2,3},{3,4},{4,5},{5,6},{6,7},{7,8},{8,9},{9,10},{10,1... | collective-permute-start | bytes 221192 | tf_op jit(solution)/shard_map/ppermute | solution.py:14
  17.8 5.9 %collective-permute-start.3 = (bf16[18,1,2048]{2,1,0:T(2,128)(2,1)S(1)}, bf16[18,1,2048]{2,1,0:T(2,128)(2,1)S(1)}, u32[]{:S(2)}, u32[]{:S(2)}) collective-permute-start(bf16[18,1,2048]{2,1,0:T(2,128)(2,1)S(1)} %get-tuple-element.177), channel_id=1, source_target_pairs={{1,0},{2,1},{3,2},{4,3},{5,4},{6,5},{7,6},{8,7},{9,8},{10,9},{11,1... | collective-permute-start | bytes 221192 | tf_op jit(solution)/shard_map/ppermute | solution.py:15
  28.3 3.0 copy-start.4
  28.3 2.9 copy-start.5
  28.3 2.9 copy-start.6
  28.3 2.9 copy-start.7
  72.5 192.0 %copy-start.11 = (s32[16]{0:T(128)S(1)}, s32[16]{0:T(128)}, u32[]{:S(2)}) copy-start(s32[16]{0:T(128)} %param.17) | copy-start | bytes 196
  72.5 251.8 %all-to-all-start = ((bf16[16,2,40960]{2,1,0:T(2,128)(2,1)}), bf16[16,2,40960]{2,1,0:T(2,128)(2,1)S(1)}, u32[]{:S(2)}, u32[]{:S(2)}) async-start(bf16[16,2,40960]{2,1,0:T(2,128)(2,1)} %reshape.54), calls=%async_computation | async-start | bytes 5242880 | tf_op jit(solution)/shard_map/all_to_all | solution.py:134
  352.8 5.6 %copy-start.3 = (bf16[3,3,32,20]{2,3,1,0:T(8,128)(2,1)S(1)}, bf16[3,3,32,20]{2,3,1,0:T(8,128)(2,1)}, u32[]{:S(2)}) copy-start(bf16[3,3,32,20]{2,3,1,0:T(8,128)(2,1)} %param.22) | copy-start | bytes 34564
  353.7 37.8 %copy-start.2 = (f32[20,32,128]{2,1,0:T(8,128)}, f32[20,32,128]{2,1,0:T(8,128)S(1)}, u32[]{:S(2)}) copy-start(f32[20,32,128]{2,1,0:T(8,128)S(1)} %multiply_reduce_fusion.2) | copy-start | bytes 983044
  354.0 5.0 %collective-permute-start.4 = (bf16[20,32,1]{2,0,1:T(8,128)(2,1)S(1)}, bf16[20,32,1]{2,0,1:T(8,128)(2,1)S(1)}, u32[]{:S(2)}, u32[]{:S(2)}) collective-permute-start(bf16[20,32,1]{2,0,1:T(8,128)(2,1)S(1)} %get-tuple-element.190), channel_id=1, source_target_pairs={{0,16},{16,32},{32,48},{48,64},{64,80},{80,96},{96,112},{112,128},... | collective-permute-start | bytes 3848 | tf_op jit(solution)/shard_map/ppermute | solution.py:14
  356.4 7.0 %collective-permute-start.5 = (bf16[20,32,1]{2,0,1:T(8,128)(2,1)S(1)}, bf16[20,32,1]{2,0,1:T(8,128)(2,1)S(1)}, u32[]{:S(2)}, u32[]{:S(2)}) collective-permute-start(bf16[20,32,1]{2,0,1:T(8,128)(2,1)S(1)} %get-tuple-element.191), channel_id=1, source_target_pairs={{16,0},{32,16},{48,32},{64,48},{80,64},{96,80},{112,96},{128,112},... | collective-permute-start | bytes 3848 | tf_op jit(solution)/shard_map/ppermute | solution.py:15
  363.5 24.5 %collective-permute-start.6 = (bf16[20,1,130]{2,0,1:T(8,128)(2,1)S(1)}, bf16[20,1,130]{2,0,1:T(8,128)(2,1)S(1)}, u32[]{:S(2)}, u32[]{:S(2)}) collective-permute-start(bf16[20,1,130]{2,0,1:T(8,128)(2,1)S(1)} %get-tuple-element.186), channel_id=1, source_target_pairs={{0,1},{1,2},{2,3},{3,4},{4,5},{5,6},{6,7},{7,8},{8,9},{9,10},{10,1... | collective-permute-start | bytes 15608 | tf_op jit(solution)/shard_map/ppermute | solution.py:14
  386.3 4.4 %collective-permute-start.7 = (bf16[20,1,130]{2,0,1:T(8,128)(2,1)S(1)}, bf16[20,1,130]{2,0,1:T(8,128)(2,1)S(1)}, u32[]{:S(2)}, u32[]{:S(2)}) collective-permute-start(bf16[20,1,130]{2,0,1:T(8,128)(2,1)S(1)} %get-tuple-element.187), channel_id=1, source_target_pairs={{1,0},{2,1},{3,2},{4,3},{5,4},{6,5},{7,6},{8,7},{9,8},{10,9},{11,1... | collective-permute-start | bytes 15608 | tf_op jit(solution)/shard_map/ppermute | solution.py:15
  391.2 1.9 copy-start.10
  392.7 6.0 %copy-start.8 = (bf16[3,3,3,32]{3,2,1,0:T(4,128)(2,1)S(1)}, bf16[3,3,3,32]{3,2,1,0:T(4,128)(2,1)}, u32[]{:S(2)}) copy-start(bf16[3,3,3,32]{3,2,1,0:T(4,128)(2,1)} %param.24) | copy-start | bytes 5188
  393.6 22.2 %copy-start.9 = (f32[3]{0:T(128)S(1)}, f32[3]{0:T(128)}, u32[]{:S(2)}) copy-start(f32[3]{0:T(128)} %param.25) | copy-start | bytes 40
  393.6 6.5 %collective-permute-start.8 = (bf16[32,32,1]{2,0,1:T(8,128)(2,1)S(1)}, bf16[32,32,1]{2,0,1:T(8,128)(2,1)S(1)}, u32[]{:S(2)}, u32[]{:S(2)}) collective-permute-start(bf16[32,32,1]{2,0,1:T(8,128)(2,1)S(1)} %get-tuple-element.188), channel_id=1, source_target_pairs={{0,16},{16,32},{32,48},{48,64},{64,80},{80,96},{96,112},{112,128},... | collective-permute-start | bytes 6152 | tf_op jit(solution)/shard_map/ppermute | solution.py:14
  396.8 7.7 %collective-permute-start.9 = (bf16[32,32,1]{2,0,1:T(8,128)(2,1)S(1)}, bf16[32,32,1]{2,0,1:T(8,128)(2,1)S(1)}, u32[]{:S(2)}, u32[]{:S(2)}) collective-permute-start(bf16[32,32,1]{2,0,1:T(8,128)(2,1)S(1)} %get-tuple-element.189), channel_id=1, source_target_pairs={{16,0},{32,16},{48,32},{64,48},{80,64},{96,80},{112,96},{128,112},... | collective-permute-start | bytes 6152 | tf_op jit(solution)/shard_map/ppermute | solution.py:15
  404.6 6.2 %collective-permute-start.10 = (bf16[32,1,130]{2,0,1:T(8,128)(2,1)S(1)}, bf16[32,1,130]{2,0,1:T(8,128)(2,1)S(1)}, u32[]{:S(2)}, u32[]{:S(2)}) collective-permute-start(bf16[32,1,130]{2,0,1:T(8,128)(2,1)S(1)} %get-tuple-element.182), channel_id=1, source_target_pairs={{0,1},{1,2},{2,3},{3,4},{4,5},{5,6},{6,7},{7,8},{8,9},{9,10},{10,1... | collective-permute-start | bytes 24968 | tf_op jit(solution)/shard_map/ppermute | solution.py:14
  409.2 4.8 %collective-permute-start.11 = (bf16[32,1,130]{2,0,1:T(8,128)(2,1)S(1)}, bf16[32,1,130]{2,0,1:T(8,128)(2,1)S(1)}, u32[]{:S(2)}, u32[]{:S(2)}) collective-permute-start(bf16[32,1,130]{2,0,1:T(8,128)(2,1)S(1)} %get-tuple-element.183), channel_id=1, source_target_pairs={{1,0},{2,1},{3,2},{4,3},{5,4},{6,5},{7,6},{8,7},{9,8},{10,9},{11,1... | collective-permute-start | bytes 24968 | tf_op jit(solution)/shard_map/ppermute | solution.py:15
where the time goes:
time: 422 us; the launch traced here: 417 us
  starting transfers between devices  243 us (58%)
  waiting for transfers between devices  83.1 us (20%)
  local copies, waits for them, and re-layouts  77.4 us (18%)
  other arithmetic  6.82 us (2%)
  matrix products  4.89 us (1%)
    all_to_all x1, starting transfers between devices, per_device(): lax.all_to_all(partial_value[None], 'depth', split_axis=3, concat_axis=0,...  192 us
    all_to_all x1, waiting for transfers between devices, per_device(): lax.all_to_all(partial_value[None], 'depth', split_axis=3, concat_axis=0,...  59.8 us
    unnamed x28, local copies, waits for them, and re-layouts  43.6 us
    ppermute x6, starting transfers between devices, padded_2(): before = lax.ppermute(last, axis, up)  41.1 us
    ppermute x6, waiting for transfers between devices, padded_2(): after = lax.ppermute(first, axis, down)  21.2 us
    while x1, local copies, waits for them, and re-layouts, per_device(): lax.fori_loop(0, active_slices[0, 0], advance, jnp.zeros((channels, row_c...  13.9 us
    all_to_all x1, local copies, waits for them, and re-layouts, per_device(): lax.all_to_all(partial_value[None], 'depth', split_axis=3, concat_axis=0,...  12.3 us
    ppermute x6, starting transfers between devices, padded_2(): after = lax.ppermute(first, axis, down)  9.7 us
  transfers between devices with their start and end apart: 13, of which 10 were waited for; matrix products, arithmetic and copies ran while one was open for 1% of the time, Pallas kernels for 0%

commit v1 on v0

v1 whole, which is shorter than its diff:
```python
import jax
import jax.numpy as jnp
from jax import lax
from jax.experimental import pallas as pl
from jax.experimental.pallas import tpu as pltpu
from jax.sharding import PartitionSpec as P

MESH = pl.DeviceIdType.MESH
F32, BF16 = jnp.float32, jnp.bfloat16

SLICES = 16
ROWS = 32
COLS = 2048
LANES = 128
TILES = 16
BANDS = 16
CLASSES = 8
CHANNELS = 20
SLOTS = 24
HIDDEN = 32
GROUPS = 4
STEP = 4
WIDE = COLS + 2 * LANES
OPTICAL = 2.0 / 256
UNIT = 32000.0
MOTION_MAX = 6.0
OWN = 2 * SLOTS
OWN_END = OWN + ROWS * SLOTS
FEATS = 1024
GAIN, BIAS, ALBEDO, MOTION = 0, 1, 2, 5


def dot(a, b):
    return jnp.dot(a, b, preferred_element_type=F32)


def dot_first(a, b):
    return lax.dot_general(a, b, (((0,), (0,)), ((), ())), preferred_element_type=F32)


def dot_last(a, b):
    return lax.dot_general(a, b, (((1,), (1,)), ((), ())), preferred_element_type=F32)


def iota(shape, dim):
    return lax.broadcasted_iota(jnp.int32, shape, dim)


def hot(mask):
    return jnp.where(mask, 1.0, 0.0).astype(F32)


def lookup(table, index):
    return jnp.take_along_axis(table, index, axis=0, mode="promise_in_bounds")


def kernel(
    vol,
    lab,
    active,
    order,
    gain,
    bias,
    albedo,
    motion,
    conv_first,
    bias_first,
    conv_second,
    bias_second,
    aovs,
    denoised,
    volp,
    labi,
    labp,
    row_tmp,
    row_send,
    rowp,
    smat,
    kvec,
    tables,
    vs,
    gx,
    gy,
    tc,
    qs,
    alpha_send,
    alpha_recv,
    front,
    front_send,
    front_recv,
    part,
    chunk_send,
    chunk_recv,
    feat,
    edge,
    edge_recv,
    corner_recv,
    first_tmp,
    first_mat,
    second_tmp,
    second_mat,
    x_first,
    hidden,
    x_second,
    load_sem,
    halo_ssem,
    halo_rsem,
    alpha_ssem,
    alpha_rsem,
    front_ssem,
    front_rsem,
    chunk_ssem,
    chunk_rsem,
    rim_ssem,
    rim_rsem,
):
    me = lax.axis_index("depth")
    lat = lax.axis_index("lat")
    right = lax.rem(me + 1, TILES)
    left = lax.rem(me + TILES - 1, TILES)
    down = lax.rem(lat + 1, BANDS)
    up = lax.rem(lat + BANDS - 1, BANDS)
    not_first = hot(me > 0)
    not_last = hot(me < TILES - 1)
    not_top = hot(lat > 0)
    not_bottom = hot(lat < BANDS - 1)

    def remote(src, dst, ssem, rsem, device):
        return pltpu.make_async_remote_copy(
            src_ref=src,
            dst_ref=dst,
            send_sem=ssem,
            recv_sem=rsem,
            device_id=device,
            device_id_type=MESH,
        )

    load_vol = pltpu.make_async_copy(
        vol, volp.at[pl.ds(1, SLICES), :, pl.ds(LANES, COLS)], load_sem.at[0]
    )
    load_lab = pltpu.make_async_copy(lab, labi, load_sem.at[1])
    load_vol.start()
    load_lab.start()

    side = jnp.zeros((SLICES + 2, ROWS, LANES), BF16)
    volp[:, :, 0:LANES] = side
    volp[:, :, LANES + COLS :] = side
    labp[:, :, 0:LANES] = side[:SLICES]
    labp[:, :, LANES + COLS :] = side[:SLICES]
    rowp[:, :, 0:LANES] = side[0:2, 0:SLICES]
    rowp[:, :, LANES + COLS :] = side[0:2, 0:SLICES]
    feat[...] = jnp.zeros_like(feat)

    barrier = pltpu.get_barrier_semaphore()

    def greet(device):
        pl.semaphore_signal(barrier, inc=1, device_id=device, device_id_type=MESH)

    def greet_peer(i, carry):
        greet((lax.rem(me + i, TILES), lat))
        return carry

    lax.fori_loop(1, TILES, greet_peer, 0)
    for row in (up, down):
        for col in (left, me, right):
            greet((col, row))

    class_of = iota((CLASSES, LANES), 0)
    sources = (
        [(gain, None), (bias, None)]
        + [(albedo, c) for c in range(3)]
        + [(motion, c) for c in range(2)]
    )
    for number, (ref, row) in enumerate(sources):
        table = jnp.zeros((CLASSES, LANES), F32)
        for k in range(CLASSES):
            value = ref[k] if row is None else ref[row, k]
            table = jnp.where(class_of == k, value, table)
        tables[number] = table
    source_col = iota((3 * LANES, 2 * LANES), 0) - LANES
    target = iota((3 * LANES, 2 * LANES), 1)
    lane = lax.rem(target, LANES)
    for g in range(GROUPS):
        delta = source_col - lane + (STEP * me + g)
        smat[g] = jnp.where(
            target < LANES, hot(delta == 0), hot(delta == 1) - hot(delta == -1)
        ).astype(BF16)
    lane8 = iota((8, LANES), 1)
    for s in range(SLICES):
        factor = jnp.where(s < active[0, 0], -OPTICAL, 0.0).astype(F32)
        kvec[s, 1] = jnp.zeros((8, LANES), F32) + factor
        kvec[s, 0] = jnp.where(lane8 >= STEP * me + s // STEP, factor, 0.0)

    first_tmp[...] = jnp.zeros_like(first_tmp)
    second_tmp[...] = jnp.zeros_like(second_tmp)
    for dc in range(3):
        base = jnp.zeros((HIDDEN, 2 * LANES), F32)
        base2 = jnp.zeros((8, 3 * LANES), F32)
        for dr in range(3):
            first_tmp[:, 0:CHANNELS] = conv_first[dr, dc].astype(F32)
            wide = first_tmp[...]
            base = base + (pltpu.roll(wide, SLOTS * dr, 1) if dr else wide)
            second_tmp[0:3, 0:HIDDEN] = conv_second[dr, dc].astype(F32)
            wide = second_tmp[...]
            base2 = base2 + (pltpu.roll(wide, HIDDEN * dr, 1) if dr else wide)
        for i in range(8):
            moved = pltpu.roll(base, SLOTS * i, 1) if i else base
            first_mat[dc, i * HIDDEN : (i + 1) * HIDDEN, :] = moved.astype(BF16)
            moved = pltpu.roll(base2, HIDDEN * i, 1) if i else base2
            for c in range(3):
                second_mat[dc, c * 8 + i : c * 8 + i + 1, :] = moved[c : c + 1]

    load_vol.wait()
    pl.semaphore_wait(barrier, TILES - 1 + 6)

    inner = pl.ds(LANES, COLS)
    halo = [
        remote(
            volp.at[SLICES, :, inner],
            volp.at[0, :, inner],
            halo_ssem.at[0],
            halo_rsem.at[0],
            (right, lat),
        ),
        remote(
            volp.at[1, :, inner],
            volp.at[SLICES + 1, :, inner],
            halo_ssem.at[1],
            halo_rsem.at[1],
            (left, lat),
        ),
        remote(
            row_send.at[1],
            rowp.at[0, :, inner],
            halo_ssem.at[2],
            halo_rsem.at[2],
            (me, down),
        ),
        remote(
            row_send.at[0],
            rowp.at[1, :, inner],
            halo_ssem.at[3],
            halo_rsem.at[3],
            (me, up),
        ),
    ]
    halo[0].start()
    halo[1].start()
    for end in range(2):
        for s in range(SLICES):
            rows = volp[s + 1, 16 * end : 16 * end + 16, LANES : LANES + COLS].astype(F32)
            row_tmp[s : s + 1, :] = rows[15:16] if end else rows[0:1]
        row_send[end] = row_tmp[...].astype(BF16)
    halo[2].start()
    halo[3].start()

    load_lab.wait()

    def convert(s, carry):
        labp[s, :, LANES : LANES + COLS] = labi[s].astype(F32).astype(BF16)
        return carry

    lax.fori_loop(0, SLICES, convert, 0)

    def alpha_copy(j):
        return remote(
            alpha_send.at[j],
            alpha_recv.at[me],
            alpha_ssem.at[j],
            alpha_rsem.at[me],
            (j, lat),
        )

    def alpha_arrival(j):
        return remote(
            alpha_send.at[j],
            alpha_recv.at[j],
            alpha_ssem.at[j],
            alpha_rsem.at[j],
            (j, lat),
        )

    def window(j):
        return pl.ds(pl.multiple_of(j * LANES, LANES), 3 * LANES)

    def opacities(j, carry):
        through = [jnp.ones((8, LANES), F32) for _ in range(4)]
        edge_tile = jnp.minimum(j, 1)
        for g in range(GROUPS):
            first = STEP * g
            block = volp[1 + first : 1 + first + STEP, :, window(j)]
            moved = dot(block.reshape(STEP * ROWS, 3 * LANES), smat[g])
            block = labp[first : first + STEP, :, window(j)]
            classes = dot(block.reshape(STEP * ROWS, 3 * LANES), smat[g, :, 0:LANES])
            classes = classes.astype(jnp.int32)
            vs[j, g, 1 : 1 + STEP] = moved[:, :LANES].reshape(STEP, ROWS, LANES)
            gx[j, first : first + STEP] = moved[:, LANES:].reshape(STEP, ROWS, LANES)
            qs[j, first : first + STEP] = classes.reshape(STEP, ROWS, LANES)
            for i in range(STEP):
                factor = kvec[first + i, edge_tile]
                for rb in range(4):
                    at = i * ROWS + rb * 8
                    q = classes[at : at + 8]
                    x = lookup(tables[GAIN], q) * moved[at : at + 8, :LANES]
                    x = x + lookup(tables[BIAS], q)
                    t = jnp.exp(factor * jnp.log(1.0 + jnp.exp(x)))
                    tc[j, first + i, rb * 8 : rb * 8 + 8] = t
                    through[rb] = through[rb] * t
        alpha_send[j] = (1.0 - jnp.concatenate(through, axis=0)).astype(BF16)

        @pl.when(j != me)
        def _():
            alpha_copy(j).start()

        return carry

    lax.fori_loop(0, TILES, opacities, 0)
    alpha_recv[me] = alpha_send[me]

    for copy in halo:
        copy.wait()

    def boundary(j, carry):
        for g in range(GROUPS):
            shift = smat[g, :, 0:LANES]
            below = dot(volp[STEP * g, :, window(j)], shift)
            above = dot(volp[STEP * g + STEP + 1, :, window(j)], shift)
            vs[j, g, 0] = below * not_first if g == 0 else below
            vs[j, g, STEP + 1] = above * not_last if g == GROUPS - 1 else above
            over = dot(rowp[0, :, window(j)], shift) * not_top
            under = dot(rowp[1, :, window(j)], shift) * not_bottom
            for i in range(STEP):
                s = STEP * g + i
                center = vs[j, g, 1 + i]
                before = jnp.concatenate([over[s : s + 1], center[:-1]], axis=0)
                after = jnp.concatenate([center[1:], under[s : s + 1]], axis=0)
                gy[j, s] = after - before
        return carry

    lax.fori_loop(0, TILES, boundary, 0)

    def wait_alpha(i, carry):
        alpha_arrival(lax.rem(me + i, TILES)).wait_recv()
        return carry

    lax.fori_loop(1, TILES, wait_alpha, 0)
    run = jnp.ones((ROWS, LANES), F32)
    for j in range(TILES):
        front[j] = run
        run = run * (1.0 - alpha_recv[order[j]].astype(F32))

    def front_copy(k):
        return remote(
            front_send.at[k],
            front_recv.at[me],
            front_ssem.at[k],
            front_rsem.at[me],
            (k, lat),
        )

    def front_arrival(k):
        return remote(
            front_send.at[k],
            front_recv.at[k],
            front_ssem.at[k],
            front_rsem.at[k],
            (k, lat),
        )

    def send_front(k, carry):
        rank = jnp.int32(0)
        for j in range(TILES):
            rank = jnp.where(order[j] == k, j, rank)
        front_send[k] = jnp.round(front[rank] * UNIT).astype(jnp.int32).astype(jnp.int16)

        @pl.when(k != me)
        def _():
            front_copy(k).start()

        return carry

    lax.fori_loop(0, TILES, send_front, 0)
    front_recv[me] = front_send[me]

    def chunk_copy(i, device):
        return remote(
            chunk_send.at[i],
            chunk_recv.at[i],
            chunk_ssem.at[i],
            chunk_rsem.at[i],
            (device, lat),
        )

    def render(tile, rb):
        r0 = pl.ds(pl.multiple_of(rb * 8, 8), 8)
        zero = jnp.zeros((8, LANES), F32)
        state = [zero] * 19
        through = zero + 1.0
        for s in range(SLICES):
            g, i = s // STEP, s % STEP
            v = vs[tile, g, i + 1, r0]
            below = vs[tile, g, i, r0]
            above = vs[tile, g, i + 2, r0]
            dx = gx[tile, s, r0]
            dy = gy[tile, s, r0]
            q = qs[tile, s, r0]
            dz = above - below
            inverse = lax.rsqrt(dx * dx + dy * dy + dz * dz + 4.0)
            later = through * tc[tile, s, r0]
            w = through - later
            through = later
            wn = w * inverse
            light = 0.288 * dx + 0.36 * dy + 0.384 * dz
            shaded = 0.4 * w + wn * jnp.maximum(light, 0.0)
            texture = 0.55 + 0.45 * jnp.tanh(below + above)
            plain = w * texture
            color = shaded * texture
            moving = w + (0.5 * w) * jnp.tanh(v)
            new = []
            tints = [lookup(tables[ALBEDO + c], q) for c in range(3)]
            new += [tint * color for tint in tints]
            new += [wn * dx, wn * dy, wn * dz]
            new += [tint * plain for tint in tints]
            new += [jnp.where(q == k, w, 0.0) for k in range(CLASSES - 1)]
            new += [lookup(tables[MOTION + c], q) * moving for c in range(2)]
            state = [a + b for a, b in zip(state, new)] + state[len(new) :]
        opacity = 1.0 - through
        covered = state[9:16]
        last = opacity - sum(covered[1:], covered[0])
        final = state[0:3] + [opacity] + state[3:9] + covered + [last] + state[16:18]
        for c in range(CHANNELS):
            part[c, r0] = final[c]

    def codes(tile):
        scale = front_recv[tile].astype(jnp.int32).astype(F32)[None]
        image = part[...].astype(BF16).astype(F32)
        units = jnp.concatenate(
            [image[0:18] * scale, image[18:CHANNELS] * (scale * (1.0 / MOTION_MAX))], axis=0
        )
        return jnp.round(units).astype(jnp.int32)

    def tile_step(i, carry):
        half = i // 2
        odd = lax.rem(i, 2)
        distance = jnp.where(odd == 0, 8 - half, half - 7)
        tile = lax.rem(me + distance + TILES, TILES)

        def row_block(rb, inner_carry):
            render(tile, rb)
            return inner_carry

        lax.fori_loop(0, 4, row_block, 0)

        @pl.when(i == 0)
        def _():
            def wait_front(k, inner_carry):
                front_arrival(lax.rem(me + k, TILES)).wait_recv()
                return inner_carry

            lax.fori_loop(1, TILES, wait_front, 0)

        @pl.when(i < 2)
        def _():
            chunk_send[i] = codes(tile).astype(jnp.int16)

        @pl.when((i >= 2) & (i < TILES - 1))
        def _():
            chunk_copy(i - 2, right).wait_recv()
            total = codes(tile) + chunk_recv[i - 2].astype(jnp.int32)
            chunk_send[i] = total.astype(jnp.int16)

        @pl.when(i < TILES - 1)
        def _():
            chunk_copy(i, jnp.where(odd == 0, right, left)).start()

        return carry

    lax.fori_loop(0, TILES, tile_step, 0)
    chunk_copy(TILES - 3, right).wait_recv()
    chunk_copy(TILES - 2, right).wait_recv()
    summed = chunk_recv[TILES - 3].astype(jnp.int32) + chunk_recv[TILES - 2].astype(jnp.int32)
    scale = front_recv[me].astype(jnp.int32).astype(F32)[None]
    composite = part[...].astype(BF16).astype(F32) * (scale * (1.0 / UNIT)) + jnp.concatenate(
        [
            summed[0:18].astype(F32) * (1.0 / UNIT),
            summed[18:CHANNELS].astype(F32) * (MOTION_MAX / UNIT),
        ],
        axis=0,
    )
    aovs[...] = composite
    rounded = composite.astype(BF16).astype(F32)
    for c in range(CHANNELS):
        for rb in range(4):
            start = OWN + rb * 8 * SLOTS + c
            feat[pl.ds(start, 8, stride=SLOTS), :] = rounded[c, rb * 8 : rb * 8 + 8]

    pick = iota((8, LANES), 0)
    at = iota((8, LANES), 1)
    chosen = (
        ((pick == 0) & (at == LANES - 2))
        | ((pick == 1) & (at == LANES - 1))
        | ((pick == 2) & (at == 0))
        | ((pick == 3) & (at == 1))
    )
    rim = [
        remote(
            feat.at[pl.ds(OWN, OWN)],
            feat.at[pl.ds(OWN_END, OWN)],
            rim_ssem.at[0],
            rim_rsem.at[0],
            (me, up),
        ),
        remote(
            feat.at[pl.ds(OWN_END - OWN, OWN)],
            feat.at[pl.ds(0, OWN)],
            rim_ssem.at[1],
            rim_rsem.at[1],
            (me, down),
        ),
    ]
    rim[0].start()
    rim[1].start()
    edge[...] = dot_last(hot(chosen).astype(BF16), feat[OWN:OWN_END].astype(BF16))
    top = pl.ds(0, LANES)
    bottom = pl.ds(ROWS * SLOTS - LANES, LANES)
    targets = [
        (edge, edge_recv.at[0], (right, lat)),
        (edge, edge_recv.at[1], (left, lat)),
        (edge.at[:, top], corner_recv.at[0], (right, up)),
        (edge.at[:, top], corner_recv.at[1], (left, up)),
        (edge.at[:, bottom], corner_recv.at[2], (right, down)),
        (edge.at[:, bottom], corner_recv.at[3], (left, down)),
    ]
    for number, (src, dst, device) in enumerate(targets):
        copy = remote(src, dst, rim_ssem.at[2 + number], rim_rsem.at[2 + number], device)
        copy.start()
        rim.append(copy)

    n = iota((1, 6 * LANES), 1)
    tap = n // (2 * LANES) - 1
    spot = lax.rem(n, 2 * LANES)
    column = jnp.where(
        spot < LANES,
        spot + tap,
        jnp.where(
            spot == LANES, tap - 1, jnp.where(spot == LANES + 1, LANES + tap, -9)
        ),
    )
    own_shift = hot(iota((LANES, 6 * LANES), 0) == column).astype(BF16)
    k16 = iota((16, 6 * LANES), 0)
    wanted = jnp.where(
        k16 < 2, k16 - 2, jnp.where((k16 == 10) | (k16 == 11), k16 + LANES - 10, -99)
    )
    rim_shift = hot(wanted == column).astype(BF16)
    for copy in rim:
        copy.wait()

    def both(first, second):
        return jnp.concatenate([first * not_first, second * not_last], axis=0).astype(BF16)

    middle = dot_first(both(edge_recv[0], edge_recv[1]), rim_shift)
    lower = dot_first(both(corner_recv[0], corner_recv[1]), rim_shift)
    upper = dot_first(both(corner_recv[2], corner_recv[3]), rim_shift)
    own = dot(feat[...].astype(BF16), own_shift)
    pieces = [
        (0, (own[0:OWN] + upper[LANES - OWN :]) * not_top),
        (OWN, own[OWN:OWN_END] + middle),
        (OWN_END, (own[OWN_END : OWN_END + OWN] + lower[0:OWN]) * not_bottom),
        (OWN_END + OWN, own[OWN_END + OWN :]),
    ]
    for start, piece in pieces:
        for dc in range(3):
            x_first[dc, start : start + piece.shape[0], :] = piece[
                :, dc * 2 * LANES : (dc + 1) * 2 * LANES
            ].astype(BF16)

    eye = iota((HIDDEN, HIDDEN), 0) == iota((HIDDEN, HIDDEN), 1)
    bias_col = jnp.sum(jnp.where(eye, bias_first[...], 0.0), axis=1, keepdims=True)
    bias_all = jnp.concatenate([bias_col] * 8, axis=0)
    spot = iota((1, 2 * LANES), 1)
    inside = jnp.where(
        spot == LANES, not_first, jnp.where(spot == LANES + 1, not_last, 1.0)
    )
    row_of = iota((8 * HIDDEN, 1), 0) // HIDDEN
    for b in range(5):
        total = jnp.zeros((8 * HIDDEN, 2 * LANES), F32)
        for dc in range(3):
            x = x_first[dc, 8 * SLOTS * b : 8 * SLOTS * b + 2 * LANES, :]
            total = total + dot(first_mat[dc], x)
        total = jnp.maximum(total + bias_all, 0.0) * inside
        if b == 0:
            total = total * jnp.where(row_of == 0, not_top, 1.0)
        if b == 4:
            total = total * jnp.where(row_of == 1, not_bottom, 1.0)
        hidden[8 * HIDDEN * b : 8 * HIDDEN * (b + 1), :] = total.astype(BF16)

    n = iota((1, 3 * LANES), 1)
    column = lax.rem(n, LANES) + n // LANES - 1
    source = jnp.where(column < 0, LANES, jnp.where(column == LANES, LANES + 1, column))
    second_shift = hot(iota((2 * LANES, 3 * LANES), 0) == source).astype(BF16)
    moved = dot(hidden[...], second_shift)
    for dc in range(3):
        x_second[dc] = moved[:, dc * LANES : (dc + 1) * LANES].astype(BF16)
    for b in range(4):
        total = jnp.zeros((3 * 8, LANES), F32)
        for dc in range(3):
            x = x_second[dc, 8 * HIDDEN * b : 8 * HIDDEN * b + 10 * HIDDEN, :]
            total = total + dot(second_mat[dc][:, 0 : 10 * HIDDEN].astype(BF16), x)
        for c in range(3):
            rows = slice(8 * b, 8 * b + 8)
            color = aovs[c, rows] + total[8 * c : 8 * c + 8]
            denoised[c, rows] = color + bias_second[c]

    def sent(k, carry):
        other = lax.rem(me + k, TILES)
        alpha_copy(other).wait_send()
        front_copy(other).wait_send()
        chunk_copy(k - 1, right).wait_send()
        return carry

    lax.fori_loop(1, TILES, sent, 0)


def per_device(
    volume,
    labels,
    active_slices,
    view_order,
    density_gain,
    density_bias,
    albedo_table,
    motion_table,
    conv_first,
    bias_first,
    conv_second,
    bias_second,
):
    smem = pl.BlockSpec(memory_space=pltpu.SMEM)
    vmem = pl.BlockSpec(memory_space=pltpu.VMEM)
    anywhere = pl.BlockSpec(memory_space=pl.ANY)
    cells = (TILES, SLICES, ROWS, LANES)
    tile = (TILES, ROWS, LANES)
    chunk = (CHANNELS, ROWS, LANES)
    dma = pltpu.SemaphoreType.DMA
    return pl.pallas_call(
        kernel,
        out_shape=(
            jax.ShapeDtypeStruct(chunk, F32),
            jax.ShapeDtypeStruct((3, ROWS, LANES), F32),
        ),
        in_specs=[anywhere, anywhere] + [smem] * 6 + [vmem] * 3 + [smem],
        out_specs=(vmem, vmem),
        scratch_shapes=[
            pltpu.VMEM((SLICES + 2, ROWS, WIDE), BF16),
            pltpu.VMEM((SLICES, ROWS, COLS), jnp.int32),
            pltpu.VMEM((SLICES, ROWS, WIDE), BF16),
            pltpu.VMEM((SLICES, COLS), F32),
            pltpu.VMEM((2, SLICES, COLS), BF16),
            pltpu.VMEM((2, SLICES, WIDE), BF16),
            pltpu.VMEM((GROUPS, 3 * LANES, 2 * LANES), BF16),
            pltpu.VMEM((SLICES, 2, 8, LANES), F32),
            pltpu.VMEM((7, CLASSES, LANES), F32),
            pltpu.VMEM((TILES, GROUPS, STEP + 2, ROWS, LANES), F32),
            pltpu.VMEM(cells, F32),
            pltpu.VMEM(cells, F32),
            pltpu.VMEM(cells, F32),
            pltpu.VMEM(cells, jnp.int32),
            pltpu.VMEM(tile, BF16),
            pltpu.VMEM(tile, BF16),
            pltpu.VMEM(tile, F32),
            pltpu.VMEM(tile, jnp.int16),
            pltpu.VMEM(tile, jnp.int16),
            pltpu.VMEM(chunk, F32),
            pltpu.VMEM((TILES - 1,) + chunk, jnp.int16),
            pltpu.VMEM((TILES - 1,) + chunk, jnp.int16),
            pltpu.VMEM((FEATS, LANES), F32),
            pltpu.VMEM((8, ROWS * SLOTS), F32),
            pltpu.VMEM((2, 8, ROWS * SLOTS), F32),
            pltpu.VMEM((4, 8, LANES), F32),
            pltpu.VMEM((HIDDEN, 2 * LANES), F32),
            pltpu.VMEM((3, 8 * HIDDEN, 2 * LANES), BF16),
            pltpu.VMEM((8, 3 * LANES), F32),
            pltpu.VMEM((3, 24, 3 * LANES), F32),
            pltpu.VMEM((3, FEATS, 2 * LANES), BF16),
            pltpu.VMEM((40 * HIDDEN, 2 * LANES), BF16),
            pltpu.VMEM((3, 40 * HIDDEN, LANES), BF16),
            dma((2,)),
            dma((4,)),
            dma((4,)),
            dma((TILES,)),
            dma((TILES,)),
            dma((TILES,)),
            dma((TILES,)),
            dma((TILES - 1,)),
            dma((TILES - 1,)),
            dma((8,)),
            dma((8,)),
        ],
        compiler_params=pltpu.CompilerParams(
            collective_id=0, has_side_effects=True, vmem_limit_bytes=60 * 1024 * 1024
        ),
    )(
        volume,
        labels,
        active_slices,
        view_order,
        density_gain,
        density_bias,
        albedo_table,
        motion_table,
        conv_first,
        bias_first.reshape(1, HIDDEN),
        conv_second,
        bias_second,
    )


def solution(mesh):
    placed = (P("depth", "lat", None),) * 2 + (P("depth", "lat"),) + (P(),) * 9
    return jax.shard_map(
        per_device,
        mesh=mesh,
        in_specs=placed,
        out_specs=(P(None, "lat", "depth"), P(None, "lat", "depth")),
        check_vma=False,
    )
```

time: 422 us -> 76.7 us (0.18); the launches traced: 417 us -> 76.4 us
  starting transfers between devices: 243 us -> 0 us
  waiting for transfers between devices: 83.1 us -> 0 us
  local copies, waits for them, and re-layouts: 77.4 us -> 4.72 us
  Pallas kernels: 0 us -> 70.4 us
  other arithmetic: 6.82 us -> 0 us
  matrix products: 4.89 us -> 0 us
    all_to_all x1 -> x0, starting transfers between devices: 192 us -> none  [per_device(): lax.all_to_all(partial_value[None], 'depth', split_axis=3, concat_axis=0,...]
    pallas_call x0 -> x1, Pallas kernels: none -> 70.4 us  [per_device(): pl.pallas_call(kernel, out_shape=(jax.ShapeDtypeStruct(chunk, F32), jax.S...]
    all_to_all x1 -> x0, waiting for transfers between devices: 59.8 us -> none  [per_device(): lax.all_to_all(partial_value[None], 'depth', split_axis=3, concat_axis=0,...]
    ppermute x12 -> x0, starting transfers between devices: 50.8 us -> none  [the longest x6 41.1 us: padded_2(): before = lax.ppermute(last, axis, up)]
    unnamed x28 -> x3, local copies, waits for them, and re-layouts: 43.6 us -> 4.72 us
    ppermute x12 -> x0, waiting for transfers between devices: 23.3 us -> none  [the longest x6 21.2 us: padded_2(): after = lax.ppermute(first, axis, down)]
    while x1 -> x0, local copies, waits for them, and re-layouts: 13.9 us -> none  [per_device(): lax.fori_loop(0, active_slices[0, 0], advance, jnp.zeros((channels, row_c...]
    all_to_all x1 -> x0, local copies, waits for them, and re-layouts: 12.3 us -> none  [per_device(): lax.all_to_all(partial_value[None], 'depth', split_axis=3, concat_axis=0,...]
  transfers between devices with their start and end apart: 13 -> 0, of which waited for: 10 -> 0; matrix products, arithmetic and copies ran while one was open for 1% -> 0% of each run, Pallas kernels for 0% -> 0%
where the time goes in v1:
time: 76.7 us; the launch traced here: 76.4 us
  Pallas kernels  70.4 us (92%)
  local copies, waits for them, and re-layouts  4.72 us (6%)
  between operations  1.29 us (2%)
    pallas_call x1, Pallas kernels, per_device(): pl.pallas_call(kernel, out_shape=(jax.ShapeDtypeStruct(chunk, F32), jax.S...  70.4 us
    unnamed x3, local copies, waits for them, and re-layouts  4.72 us

profile of v1, /device:TPU:1, one launch (start us, length us, event | category | flops | bytes accessed | tf_op | source)
XLA Modules:
  0.0 76.4 jit_solution(14779724692517809563)
XLA Ops:
  1.3 1.6 %copy.14.conv_first = bf16[3,3,32,20]{3,2,1,0:T(8,128)(2,1)} copy(bf16[3,3,32,20]{2,3,1,0:T(8,128)(2,1)} %param.20) | data formatting | bytes 23040 | tf_op args[8]
  2.9 70.4 %shard_map.131 = (f32[20,32,128]{2,1,0:T(8,128)}, f32[3,32,128]{2,1,0:T(8,128)}) custom-call(bf16[16,32,2048]{2,1,0:T(8,128)(2,1)} %vol.1, s32[16,32,2048]{2,1,0:T(8,128)} %lab.1, s32[1,1]{1,0:T(1,128)S(6)} %copy.17.active, s32[16]{0:T(128)} %order.1, f32[8]{0:T(128)} %gain.1, f32[8]{0:T(128)} %bias.1, f32[3,8]{1,0:T(4,128)} %albedo.1, f32[2,8]{1,0:T(2,128)} %motion.1, ...), custom_call_target="tpu_custom_call" | custom-call | tf_op jit(solution)/shard_map/pallas_call | solution.py:645
  73.3 1.7 %copy.18 = f32[20,32,128]{2,1,0:T(8,128)} copy(f32[20,32,128]{2,1,0:T(8,128)} %get-tuple-element.4) | data formatting | bytes 655360
  75.0 1.4 %copy.19 = f32[3,32,128]{2,1,0:T(8,128)} copy(f32[3,32,128]{2,1,0:T(8,128)} %get-tuple-element.5) | data formatting | bytes 98304

commit v2 on v1

--- a/solution.py
+++ b/solution.py
@@ -24,6 +24,8 @@
 OPTICAL = 2.0 / 256
 UNIT = 32000.0
 MOTION_MAX = 6.0
+HALF = 16
+BODY = slice(8, 8 + ROWS)
 OWN = 2 * SLOTS
 OWN_END = OWN + ROWS * SLOTS
 FEATS = 1024
@@ -80,7 +82,6 @@
     tables,
     vs,
     gx,
-    gy,
     tc,
     qs,
     alpha_send,
@@ -102,6 +103,9 @@
     x_first,
     hidden,
     x_second,
+    own_shift,
+    rim_shift,
+    second_shift,
     load_sem,
     halo_ssem,
     halo_rsem,
@@ -191,25 +195,6 @@
         kvec[s, 1] = jnp.zeros((8, LANES), F32) + factor
         kvec[s, 0] = jnp.where(lane8 >= STEP * me + s // STEP, factor, 0.0)
 
-    first_tmp[...] = jnp.zeros_like(first_tmp)
-    second_tmp[...] = jnp.zeros_like(second_tmp)
-    for dc in range(3):
-        base = jnp.zeros((HIDDEN, 2 * LANES), F32)
-        base2 = jnp.zeros((8, 3 * LANES), F32)
-        for dr in range(3):
-            first_tmp[:, 0:CHANNELS] = conv_first[dr, dc].astype(F32)
-            wide = first_tmp[...]
-            base = base + (pltpu.roll(wide, SLOTS * dr, 1) if dr else wide)
-            second_tmp[0:3, 0:HIDDEN] = conv_second[dr, dc].astype(F32)
-            wide = second_tmp[...]
-            base2 = base2 + (pltpu.roll(wide, HIDDEN * dr, 1) if dr else wide)
-        for i in range(8):
-            moved = pltpu.roll(base, SLOTS * i, 1) if i else base
-            first_mat[dc, i * HIDDEN : (i + 1) * HIDDEN, :] = moved.astype(BF16)
-            moved = pltpu.roll(base2, HIDDEN * i, 1) if i else base2
-            for c in range(3):
-                second_mat[dc, c * 8 + i : c * 8 + i + 1, :] = moved[c : c + 1]
-
     load_vol.wait()
     pl.semaphore_wait(barrier, TILES - 1 + 6)
 
@@ -293,7 +278,7 @@
             block = labp[first : first + STEP, :, window(j)]
             classes = dot(block.reshape(STEP * ROWS, 3 * LANES), smat[g, :, 0:LANES])
             classes = classes.astype(jnp.int32)
-            vs[j, g, 1 : 1 + STEP] = moved[:, :LANES].reshape(STEP, ROWS, LANES)
+            vs[j, g, 1 : 1 + STEP, BODY] = moved[:, :LANES].reshape(STEP, ROWS, LANES)
             gx[j, first : first + STEP] = moved[:, LANES:].reshape(STEP, ROWS, LANES)
             qs[j, first : first + STEP] = classes.reshape(STEP, ROWS, LANES)
             for i in range(STEP):
@@ -306,7 +291,8 @@
                     t = jnp.exp(factor * jnp.log(1.0 + jnp.exp(x)))
                     tc[j, first + i, rb * 8 : rb * 8 + 8] = t
                     through[rb] = through[rb] * t
-        alpha_send[j] = (1.0 - jnp.concatenate(through, axis=0)).astype(BF16)
+        opaque = 1.0 - jnp.concatenate(through, axis=0)
+        alpha_send[j] = opaque.reshape(2, HALF, LANES).astype(BF16)
 
         @pl.when(j != me)
         def _():
@@ -317,37 +303,24 @@
     lax.fori_loop(0, TILES, opacities, 0)
     alpha_recv[me] = alpha_send[me]
 
-    for copy in halo:
-        copy.wait()
-
-    def boundary(j, carry):
+    def boundary(j):
         for g in range(GROUPS):
-            shift = smat[g, :, 0:LANES]
-            below = dot(volp[STEP * g, :, window(j)], shift)
-            above = dot(volp[STEP * g + STEP + 1, :, window(j)], shift)
-            vs[j, g, 0] = below * not_first if g == 0 else below
-            vs[j, g, STEP + 1] = above * not_last if g == GROUPS - 1 else above
-            over = dot(rowp[0, :, window(j)], shift) * not_top
-            under = dot(rowp[1, :, window(j)], shift) * not_bottom
+            lines = [volp[STEP * g, :, window(j)], volp[STEP * g + STEP + 1, :, window(j)]]
+            lines += [rowp[0, :, window(j)], rowp[1, :, window(j)]]
+            moved = dot(jnp.concatenate(lines, axis=0), smat[g, :, 0:LANES])
+            below, above = moved[0:ROWS], moved[ROWS : 2 * ROWS]
+            vs[j, g, 0, BODY] = below * not_first if g == 0 else below
+            vs[j, g, STEP + 1, BODY] = above * not_last if g == GROUPS - 1 else above
+            over = moved[2 * ROWS : 2 * ROWS + SLICES] * not_top
+            under = moved[2 * ROWS + SLICES :] * not_bottom
             for i in range(STEP):
                 s = STEP * g + i
-                center = vs[j, g, 1 + i]
-                before = jnp.concatenate([over[s : s + 1], center[:-1]], axis=0)
-                after = jnp.concatenate([center[1:], under[s : s + 1]], axis=0)
-                gy[j, s] = after - before
-        return carry
-
-    lax.fori_loop(0, TILES, boundary, 0)
+                vs[j, g, 1 + i, 7:8] = over[s : s + 1]
+                vs[j, g, 1 + i, 8 + ROWS : 9 + ROWS] = under[s : s + 1]
 
     def wait_alpha(i, carry):
         alpha_arrival(lax.rem(me + i, TILES)).wait_recv()
         return carry
-
-    lax.fori_loop(1, TILES, wait_alpha, 0)
-    run = jnp.ones((ROWS, LANES), F32)
-    for j in range(TILES):
-        front[j] = run
-        run = run * (1.0 - alpha_recv[order[j]].astype(F32))
 
     def front_copy(k):
         return remote(
@@ -379,30 +352,38 @@
 
         return carry
 
-    lax.fori_loop(0, TILES, send_front, 0)
-    front_recv[me] = front_send[me]
-
-    def chunk_copy(i, device):
+    def exchange_fronts():
+        lax.fori_loop(1, TILES, wait_alpha, 0)
+        run = jnp.ones((2, HALF, LANES), F32)
+        for j in range(TILES):
+            front[j] = run
+            run = run * (1.0 - alpha_recv[order[j]].astype(F32))
+        lax.fori_loop(0, TILES, send_front, 0)
+        front_recv[me] = front_send[me]
+
+    def chunk_copy(i, h, device):
         return remote(
-            chunk_send.at[i],
-            chunk_recv.at[i],
-            chunk_ssem.at[i],
-            chunk_rsem.at[i],
+            chunk_send.at[i, h],
+            chunk_recv.at[i, h],
+            chunk_ssem.at[i, h],
+            chunk_rsem.at[i, h],
             (device, lat),
         )
 
-    def render(tile, rb):
-        r0 = pl.ds(pl.multiple_of(rb * 8, 8), 8)
+    def render(tile, buffer, h, rb):
+        first = h * HALF + rb * 8
+        r0 = pl.ds(pl.multiple_of(first, 8), 8)
+        here = pl.ds(pl.multiple_of(first + 8, 8), 8)
         zero = jnp.zeros((8, LANES), F32)
         state = [zero] * 19
         through = zero + 1.0
         for s in range(SLICES):
             g, i = s // STEP, s % STEP
-            v = vs[tile, g, i + 1, r0]
-            below = vs[tile, g, i, r0]
-            above = vs[tile, g, i + 2, r0]
+            v = vs[tile, g, i + 1, here]
+            below = vs[tile, g, i, here]
+            above = vs[tile, g, i + 2, here]
             dx = gx[tile, s, r0]
-            dy = gy[tile, s, r0]
+            dy = vs[tile, g, i + 1, pl.ds(first + 9, 8)] - vs[tile, g, i + 1, pl.ds(first + 7, 8)]
             q = qs[tile, s, r0]
             dz = above - below
             inverse = lax.rsqrt(dx * dx + dy * dy + dz * dz + 4.0)
@@ -429,70 +410,128 @@
         last = opacity - sum(covered[1:], covered[0])
         final = state[0:3] + [opacity] + state[3:9] + covered + [last] + state[16:18]
         for c in range(CHANNELS):
-            part[c, r0] = final[c]
-
-    def codes(tile):
-        scale = front_recv[tile].astype(jnp.int32).astype(F32)[None]
-        image = part[...].astype(BF16).astype(F32)
-        units = jnp.concatenate(
+            part[buffer, h, c, pl.ds(pl.multiple_of(rb * 8, 8), 8)] = final[c]
+
+    def scaled(i, h, factor):
+        image = part[lax.rem(i, 2), h].astype(BF16).astype(F32)
+        scale = front_recv[tile_of(i), h].astype(jnp.int32).astype(F32)[None] * factor
+        return jnp.concatenate(
             [image[0:18] * scale, image[18:CHANNELS] * (scale * (1.0 / MOTION_MAX))], axis=0
         )
-        return jnp.round(units).astype(jnp.int32)
+
+    def tile_of(i):
+        distance = jnp.where(lax.rem(i, 2) == 0, 8 - i // 2, i // 2 - 7)
+        return lax.rem(me + distance + TILES, TILES)
+
+    def onward(i, h):
+        @pl.when(i < 2)
+        def _():
+            chunk_send[i, h] = jnp.round(scaled(i, h, 1.0)).astype(jnp.int32).astype(jnp.int16)
+
+        @pl.when(i >= 2)
+        def _():
+            own = jnp.round(scaled(i, h, 1.0)).astype(jnp.int32)
+            chunk_copy(i - 2, h, right).wait_recv()
+            total = own + chunk_recv[i - 2, h].astype(jnp.int32)
+            chunk_send[i, h] = total.astype(jnp.int16)
+
+        chunk_copy(i, h, jnp.where(lax.rem(i, 2) == 0, right, left)).start()
 
     def tile_step(i, carry):
-        half = i // 2
-        odd = lax.rem(i, 2)
-        distance = jnp.where(odd == 0, 8 - half, half - 7)
-        tile = lax.rem(me + distance + TILES, TILES)
-
-        def row_block(rb, inner_carry):
-            render(tile, rb)
-            return inner_carry
-
-        lax.fori_loop(0, 4, row_block, 0)
+        tile = tile_of(i)
+        boundary(tile)
+
+        def half_step(h, outer_carry):
+            def row_block(rb, inner_carry):
+                render(tile, lax.rem(i, 2), h, rb)
+                return inner_carry
+
+            lax.fori_loop(0, 2, row_block, 0)
+
+            @pl.when((i == 1) & (h == 0))
+            def _():
+                def wait_front(k, inner_carry):
+                    front_arrival(lax.rem(me + k, TILES)).wait_recv()
+                    return inner_carry
+
+                lax.fori_loop(1, TILES, wait_front, 0)
+                onward(jnp.int32(0), jnp.int32(0))
+                onward(jnp.int32(0), jnp.int32(1))
+
+            @pl.when((i > 0) & (i < TILES - 1))
+            def _():
+                onward(i, h)
+
+            return outer_carry
+
+        lax.fori_loop(0, 2, half_step, 0)
 
         @pl.when(i == 0)
         def _():
-            def wait_front(k, inner_carry):
-                front_arrival(lax.rem(me + k, TILES)).wait_recv()
-                return inner_carry
-
-            lax.fori_loop(1, TILES, wait_front, 0)
-
-        @pl.when(i < 2)
-        def _():
-            chunk_send[i] = codes(tile).astype(jnp.int16)
-
-        @pl.when((i >= 2) & (i < TILES - 1))
-        def _():
-            chunk_copy(i - 2, right).wait_recv()
-            total = codes(tile) + chunk_recv[i - 2].astype(jnp.int32)
-            chunk_send[i] = total.astype(jnp.int16)
-
-        @pl.when(i < TILES - 1)
-        def _():
-            chunk_copy(i, jnp.where(odd == 0, right, left)).start()
+            exchange_fronts()
 
         return carry
 
+    for copy in halo:
+        copy.wait()
     lax.fori_loop(0, TILES, tile_step, 0)
-    chunk_copy(TILES - 3, right).wait_recv()
-    chunk_copy(TILES - 2, right).wait_recv()
-    summed = chunk_recv[TILES - 3].astype(jnp.int32) + chunk_recv[TILES - 2].astype(jnp.int32)
-    scale = front_recv[me].astype(jnp.int32).astype(F32)[None]
-    composite = part[...].astype(BF16).astype(F32) * (scale * (1.0 / UNIT)) + jnp.concatenate(
-        [
-            summed[0:18].astype(F32) * (1.0 / UNIT),
-            summed[18:CHANNELS].astype(F32) * (MOTION_MAX / UNIT),
-        ],
-        axis=0,
+
+    turn = hot(iota((CHANNELS, CHANNELS), 0) == iota((CHANNELS, CHANNELS), 1)).astype(BF16)
+    first_tmp[...] = jnp.zeros_like(first_tmp)
+    second_tmp[...] = jnp.zeros_like(second_tmp)
+    for dc in range(3):
+        base = jnp.zeros((HIDDEN, 2 * LANES), F32)
+        base2 = jnp.zeros((8, 3 * LANES), F32)
+        for dr in range(3):
+            first_tmp[:, 0:CHANNELS] = dot_first(conv_first[dr, dc], turn)
+            wide = first_tmp[...]
+            base = base + (pltpu.roll(wide, SLOTS * dr, 1) if dr else wide)
+            second_tmp[0:3, 0:HIDDEN] = conv_second[dr, dc].astype(F32)
+            wide = second_tmp[...]
+            base2 = base2 + (pltpu.roll(wide, HIDDEN * dr, 1) if dr else wide)
+        for i in range(8):
+            moved = pltpu.roll(base, SLOTS * i, 1) if i else base
+            first_mat[dc, i * HIDDEN : (i + 1) * HIDDEN, :] = moved.astype(BF16)
+            moved = pltpu.roll(base2, HIDDEN * i, 1) if i else base2
+            for c in range(3):
+                second_mat[dc, c * 8 + i : c * 8 + i + 1, :] = moved[c : c + 1]
+
+    n = iota((1, 6 * LANES), 1)
+    tap = n // (2 * LANES) - 1
+    spot = lax.rem(n, 2 * LANES)
+    column = jnp.where(
+        spot < LANES,
+        spot + tap,
+        jnp.where(
+            spot == LANES, tap - 1, jnp.where(spot == LANES + 1, LANES + tap, -9)
+        ),
     )
-    aovs[...] = composite
-    rounded = composite.astype(BF16).astype(F32)
-    for c in range(CHANNELS):
-        for rb in range(4):
-            start = OWN + rb * 8 * SLOTS + c
-            feat[pl.ds(start, 8, stride=SLOTS), :] = rounded[c, rb * 8 : rb * 8 + 8]
+    own_shift[...] = hot(iota((LANES, 6 * LANES), 0) == column).astype(BF16)
+    k16 = iota((16, 6 * LANES), 0)
+    wanted = jnp.where(
+        k16 < 2, k16 - 2, jnp.where((k16 == 10) | (k16 == 11), k16 + LANES - 10, -99)
+    )
+    rim_shift[...] = hot(wanted == column).astype(BF16)
+    n = iota((1, 3 * LANES), 1)
+    column = lax.rem(n, LANES) + n // LANES - 1
+    source = jnp.where(column < 0, LANES, jnp.where(column == LANES, LANES + 1, column))
+    second_shift[...] = hot(iota((2 * LANES, 3 * LANES), 0) == source).astype(BF16)
+    x_first[:, OWN_END + OWN :, :] = jnp.zeros((3, FEATS - OWN_END - OWN, 2 * LANES), BF16)
+
+    for h in range(2):
+        chunk_copy(TILES - 3, h, right).wait_recv()
+        chunk_copy(TILES - 2, h, right).wait_recv()
+        summed = chunk_recv[TILES - 3, h].astype(jnp.int32)
+        summed = summed + chunk_recv[TILES - 2, h].astype(jnp.int32)
+        total = scaled(TILES - 1, h, 1.0) + summed.astype(F32)
+        for c in range(CHANNELS):
+            unit = (MOTION_MAX if c >= 18 else 1.0) / UNIT
+            for rb in range(2):
+                row = h * HALF + rb * 8
+                block = total[c, rb * 8 : rb * 8 + 8] * unit
+                aovs[c, row : row + 8] = block
+                start = OWN + row * SLOTS + c
+                feat[pl.ds(start, 8, stride=SLOTS), :] = block.astype(BF16).astype(F32)
 
     pick = iota((8, LANES), 0)
     at = iota((8, LANES), 1)
@@ -536,43 +575,32 @@
         copy.start()
         rim.append(copy)
 
-    n = iota((1, 6 * LANES), 1)
-    tap = n // (2 * LANES) - 1
-    spot = lax.rem(n, 2 * LANES)
-    column = jnp.where(
-        spot < LANES,
-        spot + tap,
-        jnp.where(
-            spot == LANES, tap - 1, jnp.where(spot == LANES + 1, LANES + tap, -9)
-        ),
-    )
-    own_shift = hot(iota((LANES, 6 * LANES), 0) == column).astype(BF16)
-    k16 = iota((16, 6 * LANES), 0)
-    wanted = jnp.where(
-        k16 < 2, k16 - 2, jnp.where((k16 == 10) | (k16 == 11), k16 + LANES - 10, -99)
-    )
-    rim_shift = hot(wanted == column).astype(BF16)
+    def put(start, end, values, add):
+        for dc in range(3):
+            for side in range(2):
+                if add and dc == 1 and side == 0:
+                    continue
+                at = 2 * dc + side
+                block = values[:, at * LANES : (at + 1) * LANES].astype(BF16)
+                lanes = slice(side * LANES, (side + 1) * LANES)
+                if add:
+                    block = block + x_first[dc, start:end, lanes]
+                x_first[dc, start:end, lanes] = block
+
+    put(OWN, OWN_END, dot(feat[OWN:OWN_END].astype(BF16), own_shift[...]), False)
     for copy in rim:
         copy.wait()
 
     def both(first, second):
         return jnp.concatenate([first * not_first, second * not_last], axis=0).astype(BF16)
 
-    middle = dot_first(both(edge_recv[0], edge_recv[1]), rim_shift)
-    lower = dot_first(both(corner_recv[0], corner_recv[1]), rim_shift)
-    upper = dot_first(both(corner_recv[2], corner_recv[3]), rim_shift)
-    own = dot(feat[...].astype(BF16), own_shift)
-    pieces = [
-        (0, (own[0:OWN] + upper[LANES - OWN :]) * not_top),
-        (OWN, own[OWN:OWN_END] + middle),
-        (OWN_END, (own[OWN_END : OWN_END + OWN] + lower[0:OWN]) * not_bottom),
-        (OWN_END + OWN, own[OWN_END + OWN :]),
-    ]
-    for start, piece in pieces:
-        for dc in range(3):
-            x_first[dc, start : start + piece.shape[0], :] = piece[
-                :, dc * 2 * LANES : (dc + 1) * 2 * LANES
-            ].astype(BF16)
+    put(OWN, OWN_END, dot_first(both(edge_recv[0], edge_recv[1]), rim_shift[...]), True)
+    lower = dot_first(both(corner_recv[0], corner_recv[1]), rim_shift[...])
+    upper = dot_first(both(corner_recv[2], corner_recv[3]), rim_shift[...])
+    over = dot(feat[0:OWN].astype(BF16), own_shift[...])
+    under = dot(feat[OWN_END : OWN_END + OWN].astype(BF16), own_shift[...])
+    put(0, OWN, (over + upper[LANES - OWN :]) * not_top, False)
+    put(OWN_END, OWN_END + OWN, (under + lower[0:OWN]) * not_bottom, False)
 
     eye = iota((HIDDEN, HIDDEN), 0) == iota((HIDDEN, HIDDEN), 1)
     bias_col = jnp.sum(jnp.where(eye, bias_first[...], 0.0), axis=1, keepdims=True)
@@ -594,11 +622,7 @@
             total = total * jnp.where(row_of == 1, not_bottom, 1.0)
         hidden[8 * HIDDEN * b : 8 * HIDDEN * (b + 1), :] = total.astype(BF16)
 
-    n = iota((1, 3 * LANES), 1)
-    column = lax.rem(n, LANES) + n // LANES - 1
-    source = jnp.where(column < 0, LANES, jnp.where(column == LANES, LANES + 1, column))
-    second_shift = hot(iota((2 * LANES, 3 * LANES), 0) == source).astype(BF16)
-    moved = dot(hidden[...], second_shift)
+    moved = dot(hidden[...], second_shift[...])
     for dc in range(3):
         x_second[dc] = moved[:, dc * LANES : (dc + 1) * LANES].astype(BF16)
     for b in range(4):
@@ -615,7 +639,8 @@
         other = lax.rem(me + k, TILES)
         alpha_copy(other).wait_send()
         front_copy(other).wait_send()
-        chunk_copy(k - 1, right).wait_send()
+        chunk_copy(k - 1, 0, right).wait_send()
+        chunk_copy(k - 1, 1, right).wait_send()
         return carry
 
     lax.fori_loop(1, TILES, sent, 0)
@@ -639,8 +664,9 @@
     vmem = pl.BlockSpec(memory_space=pltpu.VMEM)
     anywhere = pl.BlockSpec(memory_space=pl.ANY)
     cells = (TILES, SLICES, ROWS, LANES)
-    tile = (TILES, ROWS, LANES)
+    tile = (TILES, 2, HALF, LANES)
     chunk = (CHANNELS, ROWS, LANES)
+    pieces = (2, CHANNELS, HALF, LANES)
     dma = pltpu.SemaphoreType.DMA
     return pl.pallas_call(
         kernel,
@@ -660,8 +686,7 @@
             pltpu.VMEM((GROUPS, 3 * LANES, 2 * LANES), BF16),
             pltpu.VMEM((SLICES, 2, 8, LANES), F32),
             pltpu.VMEM((7, CLASSES, LANES), F32),
-            pltpu.VMEM((TILES, GROUPS, STEP + 2, ROWS, LANES), F32),
-            pltpu.VMEM(cells, F32),
+            pltpu.VMEM((TILES, GROUPS, STEP + 2, ROWS + 16, LANES), F32),
             pltpu.VMEM(cells, F32),
             pltpu.VMEM(cells, F32),
             pltpu.VMEM(cells, jnp.int32),
@@ -670,9 +695,9 @@
             pltpu.VMEM(tile, F32),
             pltpu.VMEM(tile, jnp.int16),
             pltpu.VMEM(tile, jnp.int16),
-            pltpu.VMEM(chunk, F32),
-            pltpu.VMEM((TILES - 1,) + chunk, jnp.int16),
-            pltpu.VMEM((TILES - 1,) + chunk, jnp.int16),
+            pltpu.VMEM((2,) + pieces, F32),
+            pltpu.VMEM((TILES - 1,) + pieces, jnp.int16),
+            pltpu.VMEM((TILES - 1,) + pieces, jnp.int16),
             pltpu.VMEM((FEATS, LANES), F32),
             pltpu.VMEM((8, ROWS * SLOTS), F32),
             pltpu.VMEM((2, 8, ROWS * SLOTS), F32),
@@ -684,6 +709,9 @@
             pltpu.VMEM((3, FEATS, 2 * LANES), BF16),
             pltpu.VMEM((40 * HIDDEN, 2 * LANES), BF16),
             pltpu.VMEM((3, 40 * HIDDEN, LANES), BF16),
+            pltpu.VMEM((LANES, 6 * LANES), BF16),
+            pltpu.VMEM((16, 6 * LANES), BF16),
+            pltpu.VMEM((2 * LANES, 3 * LANES), BF16),
             dma((2,)),
             dma((4,)),
             dma((4,)),
@@ -691,8 +719,8 @@
             dma((TILES,)),
             dma((TILES,)),
             dma((TILES,)),
-            dma((TILES - 1,)),
-            dma((TILES - 1,)),
+            dma((TILES - 1, 2)),
+            dma((TILES - 1, 2)),
             dma((8,)),
             dma((8,)),
         ],
@@ -708,7 +736,7 @@
         density_bias,
         albedo_table,
         motion_table,
-        conv_first,
+        jnp.swapaxes(conv_first, 2, 3),
         bias_first.reshape(1, HIDDEN),
         conv_second,
         bias_second,

time: 76.7 us -> 68.5 us (0.89)
  Pallas kernels: 70.4 us -> 63.9 us
  local copies, waits for them, and re-layouts: 4.72 us -> 3.14 us
    pallas_call x1, Pallas kernels: 70.4 us -> 63.9 us  [per_device(): pl.pallas_call(kernel, out_shape=(jax.ShapeDtypeStruct(chunk, F32), jax.S...]
    unnamed x3 -> x2, local copies, waits for them, and re-layouts: 4.72 us -> 3.14 us
where the time goes in v2:
time: 68.5 us; the launch traced here: 68.3 us
  Pallas kernels  63.9 us (93%)
  local copies, waits for them, and re-layouts  3.14 us (5%)
  between operations  1.29 us (2%)
    pallas_call x1, Pallas kernels, per_device(): pl.pallas_call(kernel, out_shape=(jax.ShapeDtypeStruct(chunk, F32), jax.S...  63.9 us
    unnamed x2, local copies, waits for them, and re-layouts  3.14 us

profile of v2, /device:TPU:1, one launch (start us, length us, event | category | flops | bytes accessed | tf_op | source)
XLA Modules:
  0.0 68.3 jit_solution(8859526367724551946)
XLA Ops:
  1.3 63.9 %shard_map.131 = (f32[20,32,128]{2,1,0:T(8,128)}, f32[3,32,128]{2,1,0:T(8,128)}) custom-call(bf16[16,32,2048]{2,1,0:T(8,128)(2,1)} %vol.1, s32[16,32,2048]{2,1,0:T(8,128)} %lab.1, s32[1,1]{1,0:T(1,128)S(6)} %copy.16.active, s32[16]{0:T(128)} %order.1, f32[8]{0:T(128)} %gain.1, f32[8]{0:T(128)} %bias.1, f32[3,8]{1,0:T(4,128)} %albedo.1, f32[2,8]{1,0:T(2,128)} %motion.1, ...), custom_call_target="tpu_custom_call" | custom-call | tf_op jit(solution)/shard_map/pallas_call | solution.py:671
  65.2 1.7 %copy.17 = f32[20,32,128]{2,1,0:T(8,128)} copy(f32[20,32,128]{2,1,0:T(8,128)} %get-tuple-element.4) | data formatting | bytes 655360
  66.9 1.4 %copy.18 = f32[3,32,128]{2,1,0:T(8,128)} copy(f32[3,32,128]{2,1,0:T(8,128)} %get-tuple-element.5) | data formatting | bytes 98304

commit v3 on v2

--- a/solution.py
+++ b/solution.py
@@ -22,8 +22,15 @@
 STEP = 4
 WIDE = COLS + 2 * LANES
 OPTICAL = 2.0 / 256
+LOG2E = 1.4426950408889634
 UNIT = 32000.0
-MOTION_MAX = 6.0
+MOTION_MAX = 8.0
+CHIPS = TILES // 2
+SENT = 18
+GROUP = 18
+PIECES = 2 * SENT // GROUP
+FRONT_AT = 5
+ONWARD_AT = {0: 5, 1: 5, 2: 9, 3: 9, 4: 13, 5: 13}
 HALF = 16
 BODY = slice(8, 8 + ROWS)
 OWN = 2 * SLOTS
@@ -90,6 +97,9 @@
     front_send,
     front_recv,
     part,
+    opaque,
+    pair_send,
+    pair_recv,
     chunk_send,
     chunk_recv,
     feat,
@@ -113,6 +123,8 @@
     alpha_rsem,
     front_ssem,
     front_rsem,
+    pair_ssem,
+    pair_rsem,
     chunk_ssem,
     chunk_rsem,
     rim_ssem,
@@ -120,6 +132,11 @@
 ):
     me = lax.axis_index("depth")
     lat = lax.axis_index("lat")
+    core = lax.rem(me, 2)
+    chip = me // 2
+    sibling = me + 1 - 2 * core
+    ahead = lax.rem(me + 2, TILES)
+    behind = lax.rem(me + TILES - 2, TILES)
     right = lax.rem(me + 1, TILES)
     left = lax.rem(me + TILES - 1, TILES)
     down = lax.rem(lat + 1, BANDS)
@@ -180,7 +197,7 @@
         for k in range(CLASSES):
             value = ref[k] if row is None else ref[row, k]
             table = jnp.where(class_of == k, value, table)
-        tables[number] = table
+        tables[number] = table * LOG2E if number < ALBEDO else table
     source_col = iota((3 * LANES, 2 * LANES), 0) - LANES
     target = iota((3 * LANES, 2 * LANES), 1)
     lane = lax.rem(target, LANES)
@@ -191,7 +208,7 @@
         ).astype(BF16)
     lane8 = iota((8, LANES), 1)
     for s in range(SLICES):
-        factor = jnp.where(s < active[0, 0], -OPTICAL, 0.0).astype(F32)
+        factor = jnp.where(s < active[0, 0], -OPTICAL * LOG2E, 0.0).astype(F32)
         kvec[s, 1] = jnp.zeros((8, LANES), F32) + factor
         kvec[s, 0] = jnp.where(lane8 >= STEP * me + s // STEP, factor, 0.0)
 
@@ -273,22 +290,24 @@
         edge_tile = jnp.minimum(j, 1)
         for g in range(GROUPS):
             first = STEP * g
-            block = volp[1 + first : 1 + first + STEP, :, window(j)]
-            moved = dot(block.reshape(STEP * ROWS, 3 * LANES), smat[g])
-            block = labp[first : first + STEP, :, window(j)]
-            classes = dot(block.reshape(STEP * ROWS, 3 * LANES), smat[g, :, 0:LANES])
-            classes = classes.astype(jnp.int32)
-            vs[j, g, 1 : 1 + STEP, BODY] = moved[:, :LANES].reshape(STEP, ROWS, LANES)
-            gx[j, first : first + STEP] = moved[:, LANES:].reshape(STEP, ROWS, LANES)
+            values = volp[1 + first : 1 + first + STEP, :, window(j)]
+            marks = labp[first : first + STEP, :, window(j)]
+            both = jnp.concatenate([values, marks], axis=0)
+            moved = dot(both.reshape(2 * STEP * ROWS, 3 * LANES), smat[g, :, 0:LANES])
+            classes = moved[STEP * ROWS :].astype(jnp.int32)
+            moved = moved[: STEP * ROWS]
+            vs[j, g, 1 : 1 + STEP, BODY] = moved.reshape(STEP, ROWS, LANES)
             qs[j, first : first + STEP] = classes.reshape(STEP, ROWS, LANES)
+            slopes = dot(values.reshape(STEP * ROWS, 3 * LANES), smat[g, :, LANES : 2 * LANES])
+            gx[j, first : first + STEP] = slopes.reshape(STEP, ROWS, LANES)
             for i in range(STEP):
                 factor = kvec[first + i, edge_tile]
                 for rb in range(4):
                     at = i * ROWS + rb * 8
                     q = classes[at : at + 8]
-                    x = lookup(tables[GAIN], q) * moved[at : at + 8, :LANES]
+                    x = lookup(tables[GAIN], q) * moved[at : at + 8]
                     x = x + lookup(tables[BIAS], q)
-                    t = jnp.exp(factor * jnp.log(1.0 + jnp.exp(x)))
+                    t = jnp.exp2(factor * jnp.log(1.0 + jnp.exp2(x)))
                     tc[j, first + i, rb * 8 : rb * 8 + 8] = t
                     through[rb] = through[rb] * t
         opaque = 1.0 - jnp.concatenate(through, axis=0)
@@ -322,6 +341,9 @@
         alpha_arrival(lax.rem(me + i, TILES)).wait_recv()
         return carry
 
+    def distance_of(k):
+        return jnp.where(lax.rem(k, 2) == 0, 4 - k // 2, k // 2 - 3)
+
     def front_copy(k):
         return remote(
             front_send.at[k],
@@ -340,13 +362,15 @@
             (k, lat),
         )
 
-    def send_front(k, carry):
+    def send_front(n, carry):
+        other = lax.rem(chip - distance_of(n // 2) + CHIPS, CHIPS)
+        k = 2 * other + jnp.where(lax.rem(n, 2) == 1, core, 1 - core)
         rank = jnp.int32(0)
         for j in range(TILES):
             rank = jnp.where(order[j] == k, j, rank)
         front_send[k] = jnp.round(front[rank] * UNIT).astype(jnp.int32).astype(jnp.int16)
 
-        @pl.when(k != me)
+        @pl.when(n < TILES - 1)
         def _():
             front_copy(k).start()
 
@@ -358,24 +382,34 @@
         for j in range(TILES):
             front[j] = run
             run = run * (1.0 - alpha_recv[order[j]].astype(F32))
+        opaque[...] = 1.0 - run
         lax.fori_loop(0, TILES, send_front, 0)
         front_recv[me] = front_send[me]
 
-    def chunk_copy(i, h, device):
+    def chunk_copy(k, p):
         return remote(
-            chunk_send.at[i, h],
-            chunk_recv.at[i, h],
-            chunk_ssem.at[i, h],
-            chunk_rsem.at[i, h],
-            (device, lat),
+            chunk_send.at[k, p],
+            chunk_recv.at[k, p],
+            chunk_ssem.at[k, p],
+            chunk_rsem.at[k, p],
+            (jnp.where(lax.rem(k, 2) == 0, ahead, behind), lat),
         )
 
-    def render(tile, buffer, h, rb):
+    def pair_copy(k):
+        return remote(
+            pair_send.at[k],
+            pair_recv.at[k],
+            pair_ssem.at[k],
+            pair_rsem.at[k],
+            (sibling, lat),
+        )
+
+    def render(tile, i_tile, h, rb):
         first = h * HALF + rb * 8
         r0 = pl.ds(pl.multiple_of(first, 8), 8)
         here = pl.ds(pl.multiple_of(first + 8, 8), 8)
         zero = jnp.zeros((8, LANES), F32)
-        state = [zero] * 19
+        state = [zero] * SENT
         through = zero + 1.0
         for s in range(SLICES):
             g, i = s // STEP, s % STEP
@@ -404,71 +438,94 @@
             new += [tint * plain for tint in tints]
             new += [jnp.where(q == k, w, 0.0) for k in range(CLASSES - 1)]
             new += [lookup(tables[MOTION + c], q) * moving for c in range(2)]
-            state = [a + b for a, b in zip(state, new)] + state[len(new) :]
-        opacity = 1.0 - through
-        covered = state[9:16]
-        last = opacity - sum(covered[1:], covered[0])
-        final = state[0:3] + [opacity] + state[3:9] + covered + [last] + state[16:18]
-        for c in range(CHANNELS):
-            part[buffer, h, c, pl.ds(pl.multiple_of(rb * 8, 8), 8)] = final[c]
-
-    def scaled(i, h, factor):
-        image = part[lax.rem(i, 2), h].astype(BF16).astype(F32)
-        scale = front_recv[tile_of(i), h].astype(jnp.int32).astype(F32)[None] * factor
-        return jnp.concatenate(
-            [image[0:18] * scale, image[18:CHANNELS] * (scale * (1.0 / MOTION_MAX))], axis=0
-        )
+            state = [a + b for a, b in zip(state, new)]
+        final = state[0:16] + [a * (1.0 / MOTION_MAX) for a in state[16:18]]
+        for c in range(SENT):
+            part[i_tile, h, c, pl.ds(pl.multiple_of(rb * 8, 8), 8)] = final[c]
 
     def tile_of(i):
-        distance = jnp.where(lax.rem(i, 2) == 0, 8 - i // 2, i // 2 - 7)
-        return lax.rem(me + distance + TILES, TILES)
-
-    def onward(i, h):
-        @pl.when(i < 2)
-        def _():
-            chunk_send[i, h] = jnp.round(scaled(i, h, 1.0)).astype(jnp.int32).astype(jnp.int16)
-
-        @pl.when(i >= 2)
-        def _():
-            own = jnp.round(scaled(i, h, 1.0)).astype(jnp.int32)
-            chunk_copy(i - 2, h, right).wait_recv()
-            total = own + chunk_recv[i - 2, h].astype(jnp.int32)
-            chunk_send[i, h] = total.astype(jnp.int16)
-
-        chunk_copy(i, h, jnp.where(lax.rem(i, 2) == 0, right, left)).start()
+        kept = lax.rem(i, 2)
+        tile_chip = lax.rem(chip + distance_of(i // 2) + CHIPS, CHIPS)
+        return 2 * tile_chip + jnp.where(kept == 1, core, 1 - core)
+
+    def scaled(i, p):
+        h = p // (SENT // GROUP)
+        channels = pl.ds(GROUP * lax.rem(p, SENT // GROUP), GROUP)
+        image = part[i, h, channels].astype(BF16).astype(F32)
+        return image * front_recv[tile_of(i), h].astype(jnp.int32).astype(F32)[None]
+
+    def codes(i, p):
+        return jnp.round(scaled(i, p)).astype(jnp.int32)
+
+    def to_sibling(k):
+        front_arrival(tile_of(2 * k)).wait_recv()
+
+        def piece(p, carry):
+            pair_send[k, p] = codes(2 * k, p).astype(jnp.int16)
+            return carry
+
+        lax.fori_loop(0, PIECES, piece, 0)
+        pair_copy(k).start()
+
+    def onward(k):
+        pair_copy(k).wait_recv()
+        front_arrival(tile_of(2 * k + 1)).wait_recv()
+
+        def piece(p, carry):
+            own = codes(2 * k + 1, p) + pair_recv[k, p].astype(jnp.int32)
+
+            @pl.when(k < 2)
+            def _():
+                chunk_send[k, p] = own.astype(jnp.int16)
+
+            @pl.when(k >= 2)
+            def _():
+                chunk_copy(k - 2, p).wait_recv()
+                total = own + chunk_recv[k - 2, p].astype(jnp.int32)
+                chunk_send[k, p] = total.astype(jnp.int16)
+
+            chunk_copy(k, p).start()
+            return carry
+
+        lax.fori_loop(0, PIECES, piece, 0)
 
     def tile_step(i, carry):
         tile = tile_of(i)
         boundary(tile)
 
-        def half_step(h, outer_carry):
-            def row_block(rb, inner_carry):
-                render(tile, lax.rem(i, 2), h, rb)
-                return inner_carry
-
-            lax.fori_loop(0, 2, row_block, 0)
-
-            @pl.when((i == 1) & (h == 0))
-            def _():
-                def wait_front(k, inner_carry):
-                    front_arrival(lax.rem(me + k, TILES)).wait_recv()
-                    return inner_carry
-
-                lax.fori_loop(1, TILES, wait_front, 0)
-                onward(jnp.int32(0), jnp.int32(0))
-                onward(jnp.int32(0), jnp.int32(1))
-
-            @pl.when((i > 0) & (i < TILES - 1))
-            def _():
-                onward(i, h)
-
-            return outer_carry
-
-        lax.fori_loop(0, 2, half_step, 0)
-
-        @pl.when(i == 0)
+        def row_block(n, inner_carry):
+            render(tile, i, n // 2, lax.rem(n, 2))
+            return inner_carry
+
+        lax.fori_loop(0, 4, row_block, 0)
+
+        @pl.when(i == 1)
         def _():
             exchange_fronts()
+
+        @pl.when(i == FRONT_AT)
+        def _():
+            def early_pair(k, inner_carry):
+                to_sibling(k)
+                return inner_carry
+
+            lax.fori_loop(0, FRONT_AT // 2 + 1, early_pair, 0)
+
+        @pl.when((i > FRONT_AT) & (lax.rem(i, 2) == 0))
+        def _():
+            to_sibling(i // 2)
+
+        for at in sorted(set(ONWARD_AT.values())):
+
+            @pl.when(i == at)
+            def _(at=at):
+                steps = [k for k in ONWARD_AT if ONWARD_AT[k] == at]
+
+                def step(k, inner_carry):
+                    onward(k)
+                    return inner_carry
+
+                lax.fori_loop(steps[0], steps[-1] + 1, step, 0)
 
         return carry
 
@@ -518,20 +575,35 @@
     second_shift[...] = hot(iota((2 * LANES, 3 * LANES), 0) == source).astype(BF16)
     x_first[:, OWN_END + OWN :, :] = jnp.zeros((3, FEATS - OWN_END - OWN, 2 * LANES), BF16)
 
+    onward(jnp.int32(CHIPS - 2))
+
+    def keep(c, row, block):
+        aovs[c, row : row + 8] = block
+        start = OWN + row * SLOTS + c
+        feat[pl.ds(start, 8, stride=SLOTS), :] = block.astype(BF16).astype(F32)
+
+    pair_copy(CHIPS - 1).wait_recv()
     for h in range(2):
-        chunk_copy(TILES - 3, h, right).wait_recv()
-        chunk_copy(TILES - 2, h, right).wait_recv()
-        summed = chunk_recv[TILES - 3, h].astype(jnp.int32)
-        summed = summed + chunk_recv[TILES - 2, h].astype(jnp.int32)
-        total = scaled(TILES - 1, h, 1.0) + summed.astype(F32)
-        for c in range(CHANNELS):
-            unit = (MOTION_MAX if c >= 18 else 1.0) / UNIT
-            for rb in range(2):
-                row = h * HALF + rb * 8
-                block = total[c, rb * 8 : rb * 8 + 8] * unit
-                aovs[c, row : row + 8] = block
-                start = OWN + row * SLOTS + c
-                feat[pl.ds(start, 8, stride=SLOTS), :] = block.astype(BF16).astype(F32)
+        blocks = []
+        for piece in range(PIECES // 2):
+            p = h * (PIECES // 2) + piece
+            chunk_copy(CHIPS - 3, p).wait_recv()
+            chunk_copy(CHIPS - 2, p).wait_recv()
+            summed = pair_recv[CHIPS - 1, p].astype(jnp.int32)
+            summed = summed + chunk_recv[CHIPS - 3, p].astype(jnp.int32)
+            summed = summed + chunk_recv[CHIPS - 2, p].astype(jnp.int32)
+            total = scaled(TILES - 1, p) + summed.astype(F32)
+            blocks += [total[c] for c in range(GROUP)]
+        for rb in range(2):
+            row = h * HALF + rb * 8
+            lines = [block[rb * 8 : rb * 8 + 8] * (1.0 / UNIT) for block in blocks]
+            opacity = opaque[h, rb * 8 : rb * 8 + 8]
+            covered = lines[9:16]
+            last = opacity - sum(covered[1:], covered[0])
+            moved = [line * MOTION_MAX for line in lines[16:18]]
+            final = lines[0:3] + [opacity] + lines[3:9] + covered + [last] + moved
+            for c in range(CHANNELS):
+                keep(c, row, final[c])
 
     pick = iota((8, LANES), 0)
     at = iota((8, LANES), 1)
@@ -639,11 +711,20 @@
         other = lax.rem(me + k, TILES)
         alpha_copy(other).wait_send()
         front_copy(other).wait_send()
-        chunk_copy(k - 1, 0, right).wait_send()
-        chunk_copy(k - 1, 1, right).wait_send()
         return carry
 
+    def passed(k, carry):
+        for p in range(PIECES):
+            chunk_copy(k, p).wait_send()
+        return carry
+
+    def paired(k, carry):
+        pair_copy(k).wait_send()
+        return carry
+
     lax.fori_loop(1, TILES, sent, 0)
+    lax.fori_loop(0, CHIPS - 1, passed, 0)
+    lax.fori_loop(0, CHIPS, paired, 0)
 
 
 def per_device(
@@ -666,7 +747,7 @@
     cells = (TILES, SLICES, ROWS, LANES)
     tile = (TILES, 2, HALF, LANES)
     chunk = (CHANNELS, ROWS, LANES)
-    pieces = (2, CHANNELS, HALF, LANES)
+    pieces = (PIECES, GROUP, HALF, LANES)
     dma = pltpu.SemaphoreType.DMA
     return pl.pallas_call(
         kernel,
@@ -695,9 +776,12 @@
             pltpu.VMEM(tile, F32),
             pltpu.VMEM(tile, jnp.int16),
             pltpu.VMEM(tile, jnp.int16),
-            pltpu.VMEM((2,) + pieces, F32),
-            pltpu.VMEM((TILES - 1,) + pieces, jnp.int16),
-            pltpu.VMEM((TILES - 1,) + pieces, jnp.int16),
+            pltpu.VMEM((TILES, 2, SENT, HALF, LANES), F32),
+            pltpu.VMEM((2, HALF, LANES), F32),
+            pltpu.VMEM((CHIPS,) + pieces, jnp.int16),
+            pltpu.VMEM((CHIPS,) + pieces, jnp.int16),
+            pltpu.VMEM((CHIPS - 1,) + pieces, jnp.int16),
+            pltpu.VMEM((CHIPS - 1,) + pieces, jnp.int16),
             pltpu.VMEM((FEATS, LANES), F32),
             pltpu.VMEM((8, ROWS * SLOTS), F32),
             pltpu.VMEM((2, 8, ROWS * SLOTS), F32),
@@ -719,8 +803,10 @@
             dma((TILES,)),
             dma((TILES,)),
             dma((TILES,)),
-            dma((TILES - 1, 2)),
-            dma((TILES - 1, 2)),
+            dma((CHIPS,)),
+            dma((CHIPS,)),
+            dma((CHIPS - 1, PIECES)),
+            dma((CHIPS - 1, PIECES)),
             dma((8,)),
             dma((8,)),
         ],

time: 68.5 us -> 63.4 us (0.926)
  Pallas kernels: 63.9 us -> 58.7 us
    pallas_call x1, Pallas kernels: 63.9 us -> 58.7 us  [per_device(): pl.pallas_call(kernel, out_shape=(jax.ShapeDtypeStruct(chunk, F32), jax.S...]
where the time goes in v3:
time: 63.4 us; the launch traced here: 63.1 us
  Pallas kernels  58.7 us (93%)
  local copies, waits for them, and re-layouts  3.14 us (5%)
  between operations  1.29 us (2%)
    pallas_call x1, Pallas kernels, per_device(): pl.pallas_call(kernel, out_shape=(jax.ShapeDtypeStruct(chunk, F32), jax.S...  58.7 us
    unnamed x2, local copies, waits for them, and re-layouts  3.14 us

profile of v3, /device:TPU:1, one launch (start us, length us, event | category | flops | bytes accessed | tf_op | source)
XLA Modules:
  0.0 63.1 jit_solution(15450317276640532366)
XLA Ops:
  1.3 58.7 %shard_map.131 = (f32[20,32,128]{2,1,0:T(8,128)}, f32[3,32,128]{2,1,0:T(8,128)}) custom-call(bf16[16,32,2048]{2,1,0:T(8,128)(2,1)} %vol.1, s32[16,32,2048]{2,1,0:T(8,128)} %lab.1, s32[1,1]{1,0:T(1,128)S(6)} %copy.16.active, s32[16]{0:T(128)} %order.1, f32[8]{0:T(128)} %gain.1, f32[8]{0:T(128)} %bias.1, f32[3,8]{1,0:T(4,128)} %albedo.1, f32[2,8]{1,0:T(2,128)} %motion.1, ...), custom_call_target="tpu_custom_call" | custom-call | tf_op jit(solution)/shard_map/pallas_call | solution.py:752
  60.0 1.7 %copy.17 = f32[20,32,128]{2,1,0:T(8,128)} copy(f32[20,32,128]{2,1,0:T(8,128)} %get-tuple-element.4) | data formatting | bytes 655360
  61.7 1.4 %copy.18 = f32[3,32,128]{2,1,0:T(8,128)} copy(f32[3,32,128]{2,1,0:T(8,128)} %get-tuple-element.5) | data formatting | bytes 98304

commit v4 on v3

--- a/solution.py
+++ b/solution.py
@@ -29,8 +29,17 @@
 SENT = 18
 GROUP = 18
 PIECES = 2 * SENT // GROUP
-FRONT_AT = 5
-ONWARD_AT = {0: 5, 1: 5, 2: 9, 3: 9, 4: 13, 5: 13}
+FRONT_AT = 4
+ONWARD_AT = {
+    4: ((0, 0), (0, 1)),
+    5: ((1, 0), (1, 1)),
+    8: ((2, 0),),
+    9: ((2, 1),),
+    10: ((3, 0), (3, 1)),
+    12: ((4, 0),),
+    13: ((4, 1),),
+    14: ((5, 0), (5, 1)),
+}
 HALF = 16
 BODY = slice(8, 8 + ROWS)
 OWN = 2 * SLOTS
@@ -163,6 +172,20 @@
     load_vol.start()
     load_lab.start()
 
+    barrier = pltpu.get_barrier_semaphore()
+
+    def greet(device):
+        pl.semaphore_signal(barrier, inc=1, device_id=device, device_id_type=MESH)
+
+    def greet_peer(i, carry):
+        greet((lax.rem(me + i, TILES), lat))
+        return carry
+
+    lax.fori_loop(1, TILES, greet_peer, 0)
+    for row in (up, down):
+        for col in (left, me, right):
+            greet((col, row))
+
     side = jnp.zeros((SLICES + 2, ROWS, LANES), BF16)
     volp[:, :, 0:LANES] = side
     volp[:, :, LANES + COLS :] = side
@@ -170,21 +193,7 @@
     labp[:, :, LANES + COLS :] = side[:SLICES]
     rowp[:, :, 0:LANES] = side[0:2, 0:SLICES]
     rowp[:, :, LANES + COLS :] = side[0:2, 0:SLICES]
-    feat[...] = jnp.zeros_like(feat)
-
-    barrier = pltpu.get_barrier_semaphore()
-
-    def greet(device):
-        pl.semaphore_signal(barrier, inc=1, device_id=device, device_id_type=MESH)
-
-    def greet_peer(i, carry):
-        greet((lax.rem(me + i, TILES), lat))
-        return carry
-
-    lax.fori_loop(1, TILES, greet_peer, 0)
-    for row in (up, down):
-        for col in (left, me, right):
-            greet((col, row))
+    feat[OWN:OWN_END] = jnp.zeros((ROWS * SLOTS, LANES), F32)
 
     class_of = iota((CLASSES, LANES), 0)
     sources = (
@@ -322,20 +331,25 @@
     lax.fori_loop(0, TILES, opacities, 0)
     alpha_recv[me] = alpha_send[me]
 
-    def boundary(j):
+    def boundary(first_tile):
         for g in range(GROUPS):
-            lines = [volp[STEP * g, :, window(j)], volp[STEP * g + STEP + 1, :, window(j)]]
-            lines += [rowp[0, :, window(j)], rowp[1, :, window(j)]]
-            moved = dot(jnp.concatenate(lines, axis=0), smat[g, :, 0:LANES])
-            below, above = moved[0:ROWS], moved[ROWS : 2 * ROWS]
-            vs[j, g, 0, BODY] = below * not_first if g == 0 else below
-            vs[j, g, STEP + 1, BODY] = above * not_last if g == GROUPS - 1 else above
-            over = moved[2 * ROWS : 2 * ROWS + SLICES] * not_top
-            under = moved[2 * ROWS + SLICES :] * not_bottom
-            for i in range(STEP):
-                s = STEP * g + i
-                vs[j, g, 1 + i, 7:8] = over[s : s + 1]
-                vs[j, g, 1 + i, 8 + ROWS : 9 + ROWS] = under[s : s + 1]
+            lines = []
+            for j in (first_tile, first_tile + 1):
+                lines += [volp[STEP * g, :, window(j)], volp[STEP * g + STEP + 1, :, window(j)]]
+                lines += [rowp[0, :, window(j)], rowp[1, :, window(j)]]
+            both_tiles = dot(jnp.concatenate(lines, axis=0), smat[g, :, 0:LANES])
+            for number in range(2):
+                j = first_tile + number
+                moved = both_tiles[number * 3 * ROWS : (number + 1) * 3 * ROWS]
+                below, above = moved[0:ROWS], moved[ROWS : 2 * ROWS]
+                vs[j, g, 0, BODY] = below * not_first if g == 0 else below
+                vs[j, g, STEP + 1, BODY] = above * not_last if g == GROUPS - 1 else above
+                over = moved[2 * ROWS : 2 * ROWS + SLICES] * not_top
+                under = moved[2 * ROWS + SLICES :] * not_bottom
+                for i in range(STEP):
+                    s = STEP * g + i
+                    vs[j, g, 1 + i, 7:8] = over[s : s + 1]
+                    vs[j, g, 1 + i, 8 + ROWS : 9 + ROWS] = under[s : s + 1]
 
     def wait_alpha(i, carry):
         alpha_arrival(lax.rem(me + i, TILES)).wait_recv()
@@ -467,31 +481,24 @@
         lax.fori_loop(0, PIECES, piece, 0)
         pair_copy(k).start()
 
-    def onward(k):
-        pair_copy(k).wait_recv()
-        front_arrival(tile_of(2 * k + 1)).wait_recv()
-
-        def piece(p, carry):
-            own = codes(2 * k + 1, p) + pair_recv[k, p].astype(jnp.int32)
-
-            @pl.when(k < 2)
-            def _():
-                chunk_send[k, p] = own.astype(jnp.int16)
-
-            @pl.when(k >= 2)
-            def _():
-                chunk_copy(k - 2, p).wait_recv()
-                total = own + chunk_recv[k - 2, p].astype(jnp.int32)
-                chunk_send[k, p] = total.astype(jnp.int16)
-
-            chunk_copy(k, p).start()
-            return carry
-
-        lax.fori_loop(0, PIECES, piece, 0)
+    def onward(k, p):
+        if p == 0:
+            pair_copy(k).wait_recv()
+            front_arrival(tile_of(2 * k + 1)).wait_recv()
+        total = codes(2 * k + 1, p) + pair_recv[k, p].astype(jnp.int32)
+        if k >= 2:
+            chunk_copy(k - 2, p).wait_recv()
+            total = total + chunk_recv[k - 2, p].astype(jnp.int32)
+        chunk_send[k, p] = total.astype(jnp.int16)
+        chunk_copy(k, p).start()
 
     def tile_step(i, carry):
         tile = tile_of(i)
-        boundary(tile)
+
+        @pl.when(lax.rem(i, 2) == 0)
+        def _():
+            boundary(2 * (tile // 2))
+
 
         def row_block(n, inner_carry):
             render(tile, i, n // 2, lax.rem(n, 2))
@@ -515,17 +522,12 @@
         def _():
             to_sibling(i // 2)
 
-        for at in sorted(set(ONWARD_AT.values())):
+        for at, pieces in ONWARD_AT.items():
 
             @pl.when(i == at)
-            def _(at=at):
-                steps = [k for k in ONWARD_AT if ONWARD_AT[k] == at]
-
-                def step(k, inner_carry):
-                    onward(k)
-                    return inner_carry
-
-                lax.fori_loop(steps[0], steps[-1] + 1, step, 0)
+            def _(pieces=pieces):
+                for k, p in pieces:
+                    onward(k, p)
 
         return carry
 
@@ -575,7 +577,8 @@
     second_shift[...] = hot(iota((2 * LANES, 3 * LANES), 0) == source).astype(BF16)
     x_first[:, OWN_END + OWN :, :] = jnp.zeros((3, FEATS - OWN_END - OWN, 2 * LANES), BF16)
 
-    onward(jnp.int32(CHIPS - 2))
+    onward(CHIPS - 2, 0)
+    onward(CHIPS - 2, 1)
 
     def keep(c, row, block):
         aovs[c, row : row + 8] = block

time: 63.4 us -> 61.7 us (0.973)
  Pallas kernels: 58.7 us -> 57 us
    pallas_call x1, Pallas kernels: 58.7 us -> 57 us  [per_device(): pl.pallas_call(kernel, out_shape=(jax.ShapeDtypeStruct(chunk, F32), jax.S...]
where the time goes in v4:
time: 61.7 us; the launch traced here: 61.4 us
  Pallas kernels  57 us (92%)
  local copies, waits for them, and re-layouts  3.14 us (5%)
  between operations  1.29 us (2%)
    pallas_call x1, Pallas kernels, per_device(): pl.pallas_call(kernel, out_shape=(jax.ShapeDtypeStruct(chunk, F32), jax.S...  57 us
    unnamed x2, local copies, waits for them, and re-layouts  3.14 us

profile of v4, /device:TPU:1, one launch (start us, length us, event | category | flops | bytes accessed | tf_op | source)
XLA Modules:
  0.0 61.4 jit_solution(6678252168780548801)
XLA Ops:
  1.3 57.0 %shard_map.131 = (f32[20,32,128]{2,1,0:T(8,128)}, f32[3,32,128]{2,1,0:T(8,128)}) custom-call(bf16[16,32,2048]{2,1,0:T(8,128)(2,1)} %vol.1, s32[16,32,2048]{2,1,0:T(8,128)} %lab.1, s32[1,1]{1,0:T(1,128)S(6)} %copy.16.active, s32[16]{0:T(128)} %order.1, f32[8]{0:T(128)} %gain.1, f32[8]{0:T(128)} %bias.1, f32[3,8]{1,0:T(4,128)} %albedo.1, f32[2,8]{1,0:T(2,128)} %motion.1, ...), custom_call_target="tpu_custom_call" | custom-call | tf_op jit(solution)/shard_map/pallas_call | solution.py:755
  58.3 1.7 %copy.17 = f32[20,32,128]{2,1,0:T(8,128)} copy(f32[20,32,128]{2,1,0:T(8,128)} %get-tuple-element.4) | data formatting | bytes 655360
  60.0 1.4 %copy.18 = f32[3,32,128]{2,1,0:T(8,128)} copy(f32[3,32,128]{2,1,0:T(8,128)} %get-tuple-element.5) | data formatting | bytes 98304

commit v5 on v4

--- a/solution.py
+++ b/solution.py
@@ -30,16 +30,7 @@
 GROUP = 18
 PIECES = 2 * SENT // GROUP
 FRONT_AT = 4
-ONWARD_AT = {
-    4: ((0, 0), (0, 1)),
-    5: ((1, 0), (1, 1)),
-    8: ((2, 0),),
-    9: ((2, 1),),
-    10: ((3, 0), (3, 1)),
-    12: ((4, 0),),
-    13: ((4, 1),),
-    14: ((5, 0), (5, 1)),
-}
+ONWARD_AT = {4: ((0, 0), (0, 1)), 5: ((1, 0), (1, 1)), 8: ((2, 0),), 9: ((2, 1),), 10: ((3, 0), (3, 1)), 12: ((4, 0),), 13: ((4, 1),), 14: ((5, 0), (5, 1))}
 HALF = 16
 BODY = slice(8, 8 + ROWS)
 OWN = 2 * SLOTS
@@ -221,20 +212,19 @@
         kvec[s, 1] = jnp.zeros((8, LANES), F32) + factor
         kvec[s, 0] = jnp.where(lane8 >= STEP * me + s // STEP, factor, 0.0)
 
-    load_vol.wait()
     pl.semaphore_wait(barrier, TILES - 1 + 6)
 
     inner = pl.ds(LANES, COLS)
     halo = [
         remote(
-            volp.at[SLICES, :, inner],
+            vol.at[SLICES - 1],
             volp.at[0, :, inner],
             halo_ssem.at[0],
             halo_rsem.at[0],
             (right, lat),
         ),
         remote(
-            volp.at[1, :, inner],
+            vol.at[0],
             volp.at[SLICES + 1, :, inner],
             halo_ssem.at[1],
             halo_rsem.at[1],
@@ -257,6 +247,7 @@
     ]
     halo[0].start()
     halo[1].start()
+    load_vol.wait()
     for end in range(2):
         for s in range(SLICES):
             rows = volp[s + 1, 16 * end : 16 * end + 16, LANES : LANES + COLS].astype(F32)
@@ -535,6 +526,9 @@
         copy.wait()
     lax.fori_loop(0, TILES, tile_step, 0)
 
+    onward(CHIPS - 2, 0)
+    onward(CHIPS - 2, 1)
+
     turn = hot(iota((CHANNELS, CHANNELS), 0) == iota((CHANNELS, CHANNELS), 1)).astype(BF16)
     first_tmp[...] = jnp.zeros_like(first_tmp)
     second_tmp[...] = jnp.zeros_like(second_tmp)
@@ -577,8 +571,6 @@
     second_shift[...] = hot(iota((2 * LANES, 3 * LANES), 0) == source).astype(BF16)
     x_first[:, OWN_END + OWN :, :] = jnp.zeros((3, FEATS - OWN_END - OWN, 2 * LANES), BF16)
 
-    onward(CHIPS - 2, 0)
-    onward(CHIPS - 2, 1)
 
     def keep(c, row, block):
         aovs[c, row : row + 8] = block

time: 61.7 us -> 61.6 us (level)
  no operation moved by 1% of the time
where the time goes in v5:
time: 61.6 us; the launch traced here: 61.3 us
  Pallas kernels  56.9 us (92%)
  local copies, waits for them, and re-layouts  3.14 us (5%)
  between operations  1.29 us (2%)
    pallas_call x1, Pallas kernels, per_device(): pl.pallas_call(kernel, out_shape=(jax.ShapeDtypeStruct(chunk, F32), jax.S...  56.9 us
    unnamed x2, local copies, waits for them, and re-layouts  3.14 us

profile of v5, /device:TPU:1, one launch (start us, length us, event | category | flops | bytes accessed | tf_op | source)
XLA Modules:
  0.0 61.3 jit_solution(1393285158411934129)
XLA Ops:
  1.3 56.9 %shard_map.131 = (f32[20,32,128]{2,1,0:T(8,128)}, f32[3,32,128]{2,1,0:T(8,128)}) custom-call(bf16[16,32,2048]{2,1,0:T(8,128)(2,1)} %vol.1, s32[16,32,2048]{2,1,0:T(8,128)} %lab.1, s32[1,1]{1,0:T(1,128)S(6)} %copy.16.active, s32[16]{0:T(128)} %order.1, f32[8]{0:T(128)} %gain.1, f32[8]{0:T(128)} %bias.1, f32[3,8]{1,0:T(4,128)} %albedo.1, f32[2,8]{1,0:T(2,128)} %motion.1, ...), custom_call_target="tpu_custom_call" | custom-call | tf_op jit(solution)/shard_map/pallas_call | solution.py:747
  58.2 1.7 %copy.17 = f32[20,32,128]{2,1,0:T(8,128)} copy(f32[20,32,128]{2,1,0:T(8,128)} %get-tuple-element.4) | data formatting | bytes 655360
  59.9 1.4 %copy.18 = f32[3,32,128]{2,1,0:T(8,128)} copy(f32[3,32,128]{2,1,0:T(8,128)} %get-tuple-element.5) | data formatting | bytes 98304
